TPU v7x, 128 devices: a whole 4x4x4 slice. The times are simulated.
128 devices in a mesh: width: 4 (over y_lo, core), hidden: 32 (over y_hi, z, x).
Axes of the slice: x: 4, y: 4 (y_hi: 2, y_lo: 2; y = y_hi * 2 + y_lo), z: 4, core: 2. Of those that a mesh axis runs over, the one named last changes fastest.
Arguments:
- hidden_in: bfloat16 [512, 16384], P('hidden', 'width'), may hold values from -75 to 75
- attn_gain: bfloat16 [16384], P('width'), may hold values from 0.5 to 1.5
- mlp_gain: bfloat16 [16384], P('width'), may hold values from 0.5 to 1.5
- w_query: bfloat16 [16384, 8192], P('width', 'hidden'), may hold values from -0.046875 to 0.046875
- w_key: bfloat16 [16384, 512], P('width', 'hidden'), may hold values from -0.046875 to 0.046875
- w_value: bfloat16 [16384, 512], P('width', 'hidden'), may hold values from -0.046875 to 0.046875
- w_out: bfloat16 [8192, 16384], P('hidden', 'width'), may hold values from -0.0625 to 0.0625
- w_gate: bfloat16 [16384, 26624], P('width', 'hidden'), may hold values from -0.046875 to 0.046875
- w_up: bfloat16 [16384, 26624], P('width', 'hidden'), may hold values from -0.046875 to 0.046875
- w_down: bfloat16 [26624, 16384], P('hidden', 'width'), may hold values from -0.0390625 to 0.0390625
- key_cache: bfloat16 [512, 128, 4, 128], P(('width', 'hidden')), may hold values from -250 to 250
- value_cache: bfloat16 [512, 128, 4, 128], P(('width', 'hidden')), may hold values from -5 to 5
- lengths: int32 [512], P(('width', 'hidden')), may hold values from 16 to 128, as said below
Outputs:
- output: bfloat16 [512, 16384], P('hidden', 'width')
Inputs may be any that keep to these rules, and one draw needn't show every extreme that they name: Row r holds keys and values at slots 0 to lengths[r] - 1; its new token takes position lengths[r].
All inputs are finite; a program needn't handle non-finite values.
Results may differ from a plain program's by a relative error of at most 0.012.
Values may be sent and summed in bfloat16 or wider, within the bound.
A program may use at most 128 MiB of HBM per device.

v0:
```python
import math

import jax
import jax.numpy as jnp
from jax import lax
from jax.sharding import PartitionSpec as P

D = 16384
HEADS = 64
KV = 4
HD = 128


rope_base = 500000.0
norm_eps = 1e-05


def normalize(values, gain_vec):
    widened = values.astype(jnp.float32)
    totals = lax.psum(jnp.sum(widened * widened, axis=1), "width")
    factor = lax.rsqrt(totals / D + norm_eps)
    return (widened * factor[:, None] * gain_vec.astype(jnp.float32)[None, :]).astype(jnp.bfloat16)


def rotate(values, positions):
    half_size = values.shape[-1] // 2
    frequency = jnp.exp(
        jnp.arange(half_size, dtype=jnp.float32) * (-2.0 * math.log(rope_base) / values.shape[-1])
    )
    angles = positions.astype(jnp.float32)[:, None] * frequency[None, :]
    cosine = jnp.cos(angles)[:, None, :]
    sine_part = jnp.sin(angles)[:, None, :]
    first_half = values[..., :half_size]
    second_half = values[..., half_size:]
    return jnp.concatenate(
        [
            first_half * cosine - second_half * sine_part,
            second_half * cosine + first_half * sine_part,
        ],
        axis=-1,
    )


def attend(queries, key_fresh, value_fresh, key_cache, value_cache, lengths):
    row_count = queries.shape[0]
    group_size = HEADS // KV
    q_turned = rotate(queries.astype(jnp.float32), lengths).astype(jnp.bfloat16)
    k_turned = rotate(key_fresh.astype(jnp.float32), lengths).astype(jnp.bfloat16)
    grouped = q_turned.reshape(row_count, KV, group_size, HD)
    factor = HD ** (-0.5)
    scores = (
        jnp.einsum("rghd,rjgd->rghj", grouped, key_cache, preferred_element_type=jnp.float32)
        * factor
    )
    own_score = (
        jnp.einsum("rghd,rgd->rgh", grouped, k_turned, preferred_element_type=jnp.float32) * factor
    )
    slots = jnp.arange(key_cache.shape[1], dtype=jnp.int32)
    visible = slots[None, :] < lengths[:, None]
    scores = jnp.where(visible[:, None, None, :], scores, -jnp.inf)
    highest = jnp.maximum(jnp.max(scores, axis=-1), own_score)
    raised = jnp.exp(scores - highest[..., None])
    own_raised = jnp.exp(own_score - highest)
    totals = jnp.sum(raised, axis=-1) + own_raised
    weights = (raised / totals[..., None]).astype(jnp.bfloat16)
    own_weight = (own_raised / totals).astype(jnp.bfloat16)
    mixed = jnp.einsum("rghj,rjgd->rghd", weights, value_cache, preferred_element_type=jnp.float32)
    mixed = (
        mixed
        + own_weight.astype(jnp.float32)[..., None] * value_fresh.astype(jnp.float32)[:, :, None, :]
    )
    return mixed.reshape(row_count, HEADS * HD).astype(jnp.bfloat16)


def on_device(
    hidden_in,
    attn_gain,
    mlp_gain,
    w_query,
    w_key,
    w_value,
    w_out,
    w_gate,
    w_up,
    w_down,
    key_cache,
    value_cache,
    lengths,
):
    normed = normalize(hidden_in, attn_gain)
    block_rows = lax.all_gather(normed, "hidden", axis=0, tiled=True)
    partial_qkv = jnp.concatenate(
        [
            jnp.dot(block_rows, w_query, preferred_element_type=jnp.float32),
            jnp.dot(block_rows, w_key, preferred_element_type=jnp.float32),
            jnp.dot(block_rows, w_value, preferred_element_type=jnp.float32),
        ],
        axis=1,
    )
    summed = lax.psum_scatter(partial_qkv, "width", scatter_dimension=0, tiled=True).astype(
        jnp.bfloat16
    )
    spread = lax.all_to_all(summed, "hidden", split_axis=0, concat_axis=1, tiled=True)
    groups = lax.axis_size("hidden")
    row_count = spread.shape[0]
    pieces = spread.reshape(row_count, groups, -1)
    q_width = w_query.shape[1]
    k_width = w_key.shape[1]
    queries = pieces[:, :, :q_width].reshape(row_count, HEADS, HD)
    key_fresh = pieces[:, :, q_width : q_width + k_width].reshape(row_count, KV, HD)
    value_fresh = pieces[:, :, q_width + k_width :].reshape(row_count, KV, HD)
    attended = attend(queries, key_fresh, value_fresh, key_cache, value_cache, lengths)
    head_block = lax.all_to_all(attended, "hidden", split_axis=1, concat_axis=0, tiled=True)
    all_rows = lax.all_gather(head_block, "width", axis=0, tiled=True)
    picked = all_rows
    projected = lax.psum_scatter(
        jnp.dot(picked, w_out, preferred_element_type=jnp.float32),
        "hidden",
        scatter_dimension=0,
        tiled=True,
    )
    residual = (hidden_in.astype(jnp.float32) + projected).astype(jnp.bfloat16)
    normed_mlp = normalize(residual, mlp_gain)
    block_rows = lax.all_gather(normed_mlp, "hidden", axis=0, tiled=True)
    both_parts = jnp.concatenate(
        [
            jnp.dot(block_rows, w_gate, preferred_element_type=jnp.float32),
            jnp.dot(block_rows, w_up, preferred_element_type=jnp.float32),
        ],
        axis=1,
    )
    units = w_gate.shape[1]
    full_sums = lax.psum(both_parts.astype(jnp.bfloat16), "width").astype(jnp.float32)
    act = (jax.nn.silu(full_sums[:, :units]) * full_sums[:, units:]).astype(jnp.bfloat16)
    picked = act
    down_part = lax.psum_scatter(
        jnp.dot(picked, w_down, preferred_element_type=jnp.float32).astype(jnp.bfloat16),
        "hidden",
        scatter_dimension=0,
        tiled=True,
    ).astype(jnp.float32)
    return (residual.astype(jnp.float32) + down_part).astype(jnp.bfloat16)


def solution(mesh):
    return jax.shard_map(
        on_device,
        mesh=mesh,
        in_specs=(
            P("hidden", "width"),
            P("width"),
            P("width"),
            P("width", "hidden"),
            P("width", "hidden"),
            P("width", "hidden"),
            P("hidden", "width"),
            P("width", "hidden"),
            P("width", "hidden"),
            P("hidden", "width"),
            P(("width", "hidden"), None, None, None),
            P(("width", "hidden"), None, None, None),
            P(("width", "hidden")),
        ),
        out_specs=P("hidden", "width"),
        check_vma=False,
    )
```

profile of v0, /device:TPU:0, one launch (start us, length us, event | category | flops | bytes accessed | tf_op | source)
XLA Modules:
  0.0 730.3 jit_solution(5343689113250945578)
XLA Ops:
  6.5 0.8 convert_element_type.88
  7.4 1.0 fusion.7
  8.4 7.1 psum.21
  15.5 1.7 fusion.9
  17.3 82.5 %all-gather.3.cloned.1.call-done = bf16[512,4096]{1,0:T(8,128)(2,1)} async-done(((bf16[16,4096]{1,0:T(8,128)(2,1)}), bf16[512,4096]{1,0:T(8,128)(2,1)}) %all-gather.3.cloned.1.call-update) | async-done | bytes 4194320 | tf_op jit(solution)/shard_map/all_gather | solution.py:91
  99.7 4.3 fusion.27
  104.1 1.2 fusion.28
  105.3 1.2 fusion.29
  106.5 0.9 pad_maximum_fusion.1
  107.5 16.0 %reduce-scatter.4.cloned.1.call-done = f32[128,288]{0,1:T(8,128)} async-done(((f32[512,288]{0,1:T(8,128)}), f32[128,288]{0,1:T(8,128)}) %reduce-scatter.4.cloned.1.call-update) | async-done | bytes 147472 | tf_op jit(solution)/shard_map/reduce_scatter | solution.py:100
  123.5 0.9 convert_element_type.90
  124.6 0.7 all_to_all.24
  125.2 9.4 %all-to-all-start = ((bf16[32,4,288]{2,1,0:T(4,128)(2,1)}), bf16[32,4,288]{2,1,0:T(4,128)(2,1)S(1)}, u32[]{:S(2)}, u32[]{:S(2)}) async-start(bf16[32,4,288]{2,1,0:T(4,128)(2,1)} %all_to_all.24), calls=%async_computation.1 | async-start | bytes 196608 | tf_op jit(solution)/shard_map/all_to_all | solution.py:103
  134.8 9.8 %all-to-all-done = bf16[32,4,288]{2,1,0:T(4,128)(2,1)S(1)} async-done(((bf16[32,4,288]{2,1,0:T(4,128)(2,1)}), bf16[32,4,288]{2,1,0:T(4,128)(2,1)S(1)}, u32[]{:S(2)}, u32[]{:S(2)}) %all-to-all-start) | async-done | bytes 73760 | tf_op jit(solution)/shard_map/all_to_all | solution.py:103
  146.1 1.4 fusion.2
  147.6 13.4 %all_to_all.32 = bf16[4,32,256]{2,0,1:T(4,128)(2,1)S(1)} all-to-all(bf16[4,32,256]{2,0,1:T(4,128)(2,1)S(1)} %copy.32), channel_id=1, replica_groups=mesh['width'=4,'hidden'=32] {'hidden'}, dimensions={1} | all-to-all | bytes 131072 | tf_op jit(solution)/shard_map/all_to_all | solution.py:113
  161.0 5.8 all_gather.10
  166.8 4.5 fusion.30
  171.4 0.6 copy-done.6
  172.0 197.7 %reduce-scatter.6.cloned.1.call-done = f32[16,4096]{1,0:T(8,128)} async-done(((f32[512,4096]{1,0:T(8,128)}), f32[16,4096]{1,0:T(8,128)}) %reduce-scatter.6.cloned.1.call-update) | async-done | bytes 262160 | tf_op jit(solution)/shard_map/reduce_scatter | solution.py:116
  369.7 1.1 fusion.11
  370.8 5.7 psum.22
  376.4 0.8 fusion.13
  377.5 75.2 %all-gather.5.cloned.1.call-done = bf16[512,4096]{1,0:T(8,128)(2,1)} async-done(((bf16[16,4096]{1,0:T(8,128)(2,1)}), bf16[512,4096]{1,0:T(8,128)(2,1)}) %all-gather.5.cloned.1.call-update) | async-done | bytes 4194320 | tf_op jit(solution)/shard_map/all_gather | solution.py:124
  452.7 8.1 %convolution_convert_fusion.1 = bf16[512,832]{0,1:T(8,128)(2,1)S(1)} fusion(bf16[512,4096]{1,0:T(8,128)(2,1)} %all-gather.5.cloned.1.call-done, bf16[4096,832]{0,1:T(8,128)(2,1)} %param.21), kind=kOutput, calls=%fused_computation.4 | convolution fusion | flops 3490086912 | bytes 11862016 | tf_op jit(solution)/shard_map/dot_general | solution.py:128
  460.8 6.0 convolution_convert_fusion.2
  466.8 1.3 pad_maximum_fusion
  468.2 48.7 %all-reduce.2.cloned.1.call-done = bf16[512,1664]{0,1:T(8,128)(2,1)} async-done(((bf16[512,1664]{0,1:T(8,128)(2,1)}), bf16[512,1664]{0,1:T(8,128)(2,1)}) %all-reduce.2.cloned.1.call-update) | async-done | bytes 1703952 | tf_op jit(solution)/shard_map/psum | solution.py:133
  516.9 1.9 convert_element_type.107
  518.8 9.2 %convolution_convert_fusion = bf16[512,4096]{1,0:T(8,128)(2,1)} fusion(bf16[832,4096]{1,0:T(8,128)(2,1)} %param.22, f32[512,1664]{0,1:T(8,128)S(1)} %convert_element_type.107), kind=kOutput, calls=%fused_computation | convolution fusion | flops 3494313984 | bytes 14417920 | tf_op jit(solution)/shard_map/dot_general | solution.py:137
  528.1 193.8 %reduce-scatter.8.cloned.1.call-done = bf16[16,4096]{1,0:T(8,128)(2,1)} async-done(((bf16[512,4096]{1,0:T(8,128)(2,1)}), bf16[16,4096]{1,0:T(8,128)(2,1)}) %reduce-scatter.8.cloned.1.call-update) | async-done | bytes 131088 | tf_op jit(solution)/shard_map/reduce_scatter | solution.py:136
  721.8 1.6 fusion.14
  (54 shorter events, 2.5 us)
Async XLA Ops:
  6.5 160.3 %copy-start = (bf16[256,4096]{1,0:T(8,128)(2,1)S(1)}, bf16[256,4096]{1,0:T(8,128)(2,1)}, u32[]{:S(2)}) copy-start(bf16[256,4096]{1,0:T(8,128)(2,1)} %param.19) | copy-start | bytes 6291460
  6.5 93.2 %all-gather.3.cloned.1.call-start = ((), (), s32[]{:S(2)}) async-start(), calls=%async_computation.5 | async-start | bytes 4325376 | tf_op jit(solution)/shard_map/all_gather | solution.py:91
  17.2 86.8 %copy-start.4 = (bf16[4096,16]{0,1:T(8,128)(2,1)S(1)}, bf16[4096,16]{0,1:T(8,128)(2,1)}, u32[]{:S(2)}) copy-start(bf16[4096,16]{0,1:T(8,128)(2,1)} %param.17) | copy-start | bytes 393220
  17.2 106.3 %reduce-scatter.4.cloned.1.call-start = ((), (), s32[]{:S(2)}) async-start(), calls=%async_computation.6 | async-start | bytes 737280 | tf_op jit(solution)/shard_map/reduce_scatter | solution.py:100
  99.7 4.3 copy-start.1
  104.1 1.2 copy-start.5
  104.1 3.3 copy-start.8
  105.3 40.0 %copy-start.3 = (bf16[4,128,4,128]{3,2,1,0:T(4,128)(2,1)S(1)}, bf16[4,128,4,128]{3,2,1,0:T(4,128)(2,1)}, u32[]{:S(2)}) copy-start(bf16[4,128,4,128]{3,2,1,0:T(4,128)(2,1)} %param.23) | copy-start | bytes 1572868
  125.2 19.3 %all-to-all-start = ((bf16[32,4,288]{2,1,0:T(4,128)(2,1)}), bf16[32,4,288]{2,1,0:T(4,128)(2,1)S(1)}, u32[]{:S(2)}, u32[]{:S(2)}) async-start(bf16[32,4,288]{2,1,0:T(4,128)(2,1)} %all_to_all.24), calls=%async_computation.1 | async-start | bytes 196608 | tf_op jit(solution)/shard_map/all_to_all | solution.py:103
  134.6 235.0 %reduce-scatter.6.cloned.1.call-start = ((), (), s32[]{:S(2)}) async-start(), calls=%async_computation.7 | async-start | bytes 8650752 | tf_op jit(solution)/shard_map/reduce_scatter | solution.py:116
  171.3 0.7 copy-start.6
  171.3 198.4 %copy-start.2 = (bf16[16,4096]{1,0:T(8,128)(2,1)S(1)}, bf16[16,4096]{1,0:T(8,128)(2,1)}, u32[]{:S(2)}) copy-start(bf16[16,4096]{1,0:T(8,128)(2,1)} %param.13) | copy-start | bytes 393220
  171.3 281.3 %all-gather.5.cloned.1.call-start = ((), (), s32[]{:S(2)}) async-start(), calls=%async_computation.8 | async-start | bytes 4325376 | tf_op jit(solution)/shard_map/all_gather | solution.py:124
  377.2 139.6 %all-reduce.2.cloned.1.call-start = ((), (), s32[]{:S(2)}) async-start(), calls=%async_computation.9 | async-start | bytes 3407872 | tf_op jit(solution)/shard_map/psum | solution.py:133
  452.7 8.1 %copy-start.7 = (bf16[512,4096]{1,0:T(8,128)(2,1)S(1)}, bf16[512,4096]{1,0:T(8,128)(2,1)}, u32[]{:S(2)}) copy-start(bf16[512,4096]{1,0:T(8,128)(2,1)} %all-gather.5.cloned.1.call-done) | copy-start | bytes 12582916
  468.1 253.7 %reduce-scatter.8.cloned.1.call-start = ((), (), s32[]{:S(2)}) async-start(), calls=%async_computation.10 | async-start | bytes 4325376 | tf_op jit(solution)/shard_map/reduce_scatter | solution.py:136
Sparse Core Ops, SparseCore 0:
  17.3 82.3 all-gather.2
  107.5 15.9 reduce-scatter.3
  171.5 198.1 reduce-scatter.5
  377.4 75.2 all-gather.4
  468.2 48.5 all-reduce.1
  528.2 193.6 reduce-scatter.7
where the time goes:
time: 731 us; the launch traced here: 730 us
  waiting for transfers between devices  624 us (85%)
  matrix products  36.6 us (5%)
  blocking collectives  31.9 us (4%)
  between operations  13.7 us (2%)
  other arithmetic  12.8 us (2%)
  starting transfers between devices  9.78 us (1%)
    reduce_scatter x1, waiting for transfers between devices, on_device(): lax.psum_scatter(jnp.dot(picked, w_out, preferred_element_type=jnp.float3...  198 us
    reduce_scatter x1, waiting for transfers between devices, on_device(): lax.psum_scatter(jnp.dot(picked, w_down, preferred_element_type=jnp.float...  194 us
    all_gather x1, waiting for transfers between devices, on_device(): block_rows = lax.all_gather(normed, 'hidden', axis=0, tiled=True)  82.5 us
    all_gather x1, waiting for transfers between devices, on_device(): block_rows = lax.all_gather(normed_mlp, 'hidden', axis=0, tiled=True)  75.2 us
    psum x1, waiting for transfers between devices, on_device(): lax.psum(both_parts.astype(jnp.bfloat16), 'width').astype(jnp.float32)  48.7 us
    reduce_scatter x1, waiting for transfers between devices, on_device(): lax.psum_scatter(partial_qkv, 'width', scatter_dimension=0, tiled=True)  16 us
  transfers between devices with their start and end apart: 7, of which 7 were waited for; matrix products, arithmetic and copies ran while one was open for 0% of the time, Pallas kernels for 0%

commit v1 on v0

v1 whole, which is shorter than its diff:
```python
import functools
import math

import jax
import jax.numpy as jnp
from jax import lax
from jax.experimental import pallas as pl
from jax.experimental.pallas import tpu as pltpu
from jax.sharding import PartitionSpec as P

D = 16384
HEADS = 64
KV = 4
HD = 128
MESH = pl.DeviceIdType.MESH
F32 = jnp.float32
BF16 = jnp.bfloat16

rope_base = 500000.0
norm_eps = 1e-05

OFFS = (0, -1, 1, 2)


class Place:
    def __init__(self):
        self.w = lax.axis_index("width")
        self.h = lax.axis_index("hidden")
        self.x = lax.rem(self.h, 4)
        self.z = lax.rem(self.h // 4, 4)
        self.yh = self.h // 16
        self.core = lax.rem(self.w, 2)
        self.yl = self.w // 2
        self.partner = (self.w, lax.rem(self.h + 16, 32))
        self.core_peer = (self.w + 1 - 2 * self.core, self.h)
        self.y_peer = (lax.rem(self.w + 2, 4), self.h)
        self.far_peer = (lax.rem(self.w + 2, 4) + 1 - 2 * self.core, self.h)

    def block(self, kind, f, p, q):
        dx, dz = (p, q) if f == 0 else (q, p)
        yh = self.yh if kind == 0 else 1 - self.yh
        return yh * 16 + lax.rem(self.z + (dz + 4), 4) * 4 + lax.rem(self.x + (dx + 4), 4)

    def neighbour(self, f, phase, sgn):
        if (f ^ phase) == 0:
            return (self.w, self.block(0, 0, sgn, 0))
        return (self.w, self.block(0, 0, 0, sgn))

    def peers(self):
        return [
            self.neighbour(0, 0, 1),
            self.neighbour(0, 0, -1),
            self.neighbour(1, 0, 1),
            self.neighbour(1, 0, -1),
            self.partner,
            self.core_peer,
            self.y_peer,
            self.far_peer,
        ]


def enter(at):
    barrier = pltpu.get_barrier_semaphore()
    peers = at.peers()
    for peer in peers:
        pl.semaphore_signal(barrier, inc=1, device_id=peer, device_id_type=MESH)
    pl.semaphore_wait(barrier, len(peers))


class Link:
    def __init__(self, ssem, rsem):
        self.ssem, self.rsem, self.sent = ssem, rsem, []

    def send(self, slot, src, dst, peer):
        copy = pltpu.make_async_remote_copy(
            src_ref=src,
            dst_ref=dst,
            send_sem=self.ssem.at[slot],
            recv_sem=self.rsem.at[slot],
            device_id=peer,
            device_id_type=MESH,
        )
        copy.start()
        self.sent.append(copy)

    def wait(self, slot, dst, peer):
        pltpu.make_async_remote_copy(
            src_ref=dst,
            dst_ref=dst,
            send_sem=self.ssem.at[slot],
            recv_sem=self.rsem.at[slot],
            device_id=peer,
            device_id_type=MESH,
        ).wait_recv()

    def finish(self):
        for copy in self.sent:
            copy.wait_send()
        self.sent = []


TREE = 60


def slot_of(kind, f, phase, j, d):
    base = (kind * 2 + f) * 15
    if phase == 0:
        return base + {1: 0, -1: 1, 0: 2}[d]
    return base + 3 + OFFS.index(j) * 3 + {1: 0, -1: 1, 0: 2}[d]


def gather_stages(at, link, g, kind, f):
    half = g.shape[2] // 2
    s = 1 if (kind ^ f) == 0 else -1

    def ref(p, q):
        return g.at[at.block(kind, f, p, q), :, pl.ds(f * half, half)]

    def send(phase, j, d, p, q, sgn):
        r = ref(p, q)
        link.send(slot_of(kind, f, phase, j, d), r, r, at.neighbour(f, phase, sgn))

    def wait(phase, j, d, p, q, sgn):
        link.wait(slot_of(kind, f, phase, j, d), ref(p, q), at.neighbour(f, phase, sgn))

    def spread(j):
        send(1, j, 1, j, 0, 1)
        send(1, j, -1, j, 0, -1)

    def relay(j):
        wait(1, j, s, j, -s, s)
        send(1, j, 0, j, -s, s)
        wait(1, j, -s, j, s, -s)

    send(0, 0, 1, 0, 0, 1)
    send(0, 0, -1, 0, 0, -1)
    spread(0)
    yield
    wait(0, 0, s, -s, 0, s)
    send(0, 0, 0, -s, 0, s)
    spread(-s)
    wait(0, 0, -s, s, 0, -s)
    spread(s)
    yield
    relay(0)
    wait(0, 0, 0, 2, 0, s)
    spread(2)
    yield
    relay(-s)
    relay(s)
    yield
    relay(2)
    yield
    for j in OFFS:
        wait(1, j, 0, j, 2, s)
    yield


def run(*groups):
    for gen in groups:
        next(gen)


def gather(at, link, ylink, yslot, g):
    mine = g.at[at.h]
    theirs = g.at[at.partner[1]]
    ylink.send(yslot, mine, mine, at.partner)
    o0, o1 = (gather_stages(at, link, g, 0, f) for f in (0, 1))
    p0, p1 = (gather_stages(at, link, g, 1, f) for f in (0, 1))
    run(o0, o1)
    run(o0, o1)
    ylink.wait(yslot, theirs, at.partner)
    run(p0, p1)
    run(o0, o1)
    run(p0, p1)
    run(o0, o1)
    run(p0, p1)
    run(o0, o1)
    run(p0, p1)
    run(o0, o1)
    run(p0, p1)
    run(p0, p1)


def scatter_stages(at, link, acc, sbuf, rbuf, kind, f, result):
    half = acc.shape[2] // 2
    s = 1 if (kind ^ f) == 0 else -1

    def own(p, q):
        return acc[at.block(kind, f, p, q), :, pl.ds(f * half, half)]

    def send(phase, j, d, sgn, value):
        slot = slot_of(kind, f, phase, j, d)
        sbuf[slot] = value.astype(BF16)
        link.send(slot, sbuf.at[slot], rbuf.at[slot], at.neighbour(f, phase, sgn))

    def take(phase, j, d, sgn):
        slot = slot_of(kind, f, phase, j, d)
        link.wait(slot, rbuf.at[slot], at.neighbour(f, phase, sgn))
        return rbuf[slot].astype(F32)

    def column(j):
        return own(j, 0) + take(1, j, s, s) + take(1, j, -s, -s)

    order = (2, -s, s, 0)
    for j in order:
        send(1, j, 0, s, own(j, 2))
    for j in order:
        send(1, j, -s, -s, own(j, -s))
    yield
    for j in order:
        send(1, j, s, s, own(j, s) + take(1, j, 0, s))
    yield
    send(0, 0, 0, s, column(2))
    send(0, 0, -s, -s, column(-s))
    yield
    send(0, 0, s, s, column(s) + take(0, 0, 0, s))
    yield
    result[f] = column(0) + take(0, 0, s, s) + take(0, 0, -s, -s)
    yield


def scatter(at, link, ylink, yslot, acc, sbuf, rbuf, ysend, yrecv, emit):
    far, near = {}, {}
    p0, p1 = (scatter_stages(at, link, acc, sbuf, rbuf, 1, f, far) for f in (0, 1))
    o0, o1 = (scatter_stages(at, link, acc, sbuf, rbuf, 0, f, near) for f in (0, 1))
    run(p0, p1)
    run(o0, o1)
    run(p0, p1)
    run(p0, p1)
    run(o0, o1)
    run(p0, p1)
    run(p0, p1)
    for f in (0, 1):
        ysend[f] = far[f].astype(BF16)
        ylink.send(yslot + f, ysend.at[f], yrecv.at[f], at.partner)
    run(o0, o1)
    run(o0, o1)
    run(o0, o1)
    for f in (0, 1):
        ylink.wait(yslot + f, yrecv.at[f], at.partner)
        emit(f, near[f] + yrecv[f].astype(F32))


def width_total(at, wlink, part, nsend, nrecv):
    nsend[...] = jnp.broadcast_to(part, nsend.shape)
    for i, peer in enumerate((at.core_peer, at.y_peer, at.far_peer)):
        wlink.send(i, nsend, nrecv.at[i], peer)
    for i, peer in enumerate((at.core_peer, at.y_peer, at.far_peer)):
        wlink.wait(i, nrecv.at[i], peer)
    wlink.finish()
    total = nsend[...] + nrecv[0] + nrecv[1] + nrecv[2]
    return total[:, :1]


def normalize(at, wlink, values, gain, nsend, nrecv):
    part = jnp.sum(values * values, axis=1, keepdims=True)
    factor = lax.rsqrt(width_total(at, wlink, part, nsend, nrecv) / D + norm_eps)
    return (values * factor * gain.astype(F32)).astype(BF16)


def dot_nn(a, b):
    return jnp.dot(a, b, preferred_element_type=F32)


def dot_nt(a, b):
    return lax.dot_general(a, b, (((1,), (1,)), ((), ())), preferred_element_type=F32)


def qkv_kernel(
    hidden_ref, gain_ref, wq_hbm, wk_hbm, wv_hbm, out_ref,
    g, wq, wkv, part, msg_s, msg_r, nsend, nrecv,
    lsem, ssem, rsem, yss, yrs, wss, wrs, nss, nrs,
):
    at = Place()
    loads = [
        pltpu.make_async_copy(wq_hbm, wq, lsem.at[0]),
        pltpu.make_async_copy(wk_hbm, wkv.at[pl.ds(0, 16)], lsem.at[1]),
        pltpu.make_async_copy(wv_hbm, wkv.at[pl.ds(16, 16)], lsem.at[2]),
    ]
    for load in loads:
        load.start()
    enter(at)
    link, ylink, wlink, nlink = Link(ssem, rsem), Link(yss, yrs), Link(wss, wrs), Link(nss, nrs)
    g[at.h] = normalize(at, nlink, hidden_ref[...].astype(F32), gain_ref[...], nsend, nrecv)
    gather(at, link, ylink, 0, g)
    for load in loads:
        load.wait()
    for i in range(4):
        rows = g[pl.ds(i * 8, 8)].reshape(128, g.shape[2])
        part[i, :, pl.ds(0, 256)] = dot_nn(rows, wq[...])
        part[i, :, pl.ds(256, 32)] = dot_nt(rows, wkv[...])
    msg_s[...] = part[...].astype(BF16)
    peers = (at.core_peer, at.y_peer, at.far_peer)
    for i, peer in enumerate(peers):
        wlink.send(i, msg_s.at[peer[0]], msg_r.at[i], peer)
    total = part[at.w]
    for i, peer in enumerate(peers):
        wlink.wait(i, msg_r.at[i], peer)
        total = total + msg_r[i].astype(F32)
    out_ref[...] = total.astype(BF16)
    for each in (link, ylink, wlink):
        each.finish()


def mlp_kernel(
    att_ref, hidden_ref, gain_ref, wo_hbm, wg_hbm, wu_hbm, wd_hbm, out_ref,
    g, wo, wg, wu, wd, acc, sbuf, rbuf, ysend, yrecv, res, nsend, nrecv, pg, s1, r1, s2, r2, act,
    lsem, ssem, rsem, gss, grs, yss, yrs, wss, wrs, nss, nrs,
):
    at = Place()
    loads = [
        pltpu.make_async_copy(src, dst, lsem.at[i])
        for i, (src, dst) in enumerate(((wo_hbm, wo), (wg_hbm, wg), (wu_hbm, wu), (wd_hbm, wd)))
    ]
    for load in loads:
        load.start()
    enter(at)
    link, ylink, wlink, nlink = Link(ssem, rsem), Link(yss, yrs), Link(wss, wrs), Link(nss, nrs)
    glink = Link(gss, grs)
    width = g.shape[2]
    half = width // 2
    step = 512

    def product(a_ref, w_ref):
        def body(i, _):
            cols = pl.ds(pl.multiple_of(i * step, step), step)
            acc[:, :, cols] = dot_nn(a_ref[...], w_ref[:, cols]).reshape(32, 16, step)
            return 0

        lax.fori_loop(0, width // step, body, 0)

    loads[0].wait()
    product(att_ref, wo)

    def emit_residual(f, value):
        cols = pl.ds(f * half, half)
        res[:, cols] = (hidden_ref[:, cols].astype(F32) + value).astype(BF16)

    scatter(at, link, ylink, 0, acc, sbuf, rbuf, ysend, yrecv, emit_residual)
    link.finish()
    ylink.finish()

    g[at.h] = normalize(at, nlink, res[...].astype(F32), gain_ref[...], nsend, nrecv)
    gather(at, glink, ylink, 2, g)
    glink.finish()
    ylink.finish()

    loads[1].wait()
    loads[2].wait()

    def gate_up(i, _):
        rows = g[pl.ds(i * 8, 8)].reshape(128, width)
        for k, w in enumerate((wg, wu)):
            pg[k, i] = dot_nt(rows, w[...])
        return 0

    lax.fori_loop(0, 4, gate_up, 0)

    c, yl = at.core, at.yl
    for k in (0, 1):
        s1[k] = pg[k, pl.ds(2 * (1 - c), 2)].astype(BF16)
        wlink.send(k, s1.at[k], r1.at[k], at.core_peer)
    for k in (0, 1):
        wlink.wait(k, r1.at[k], at.core_peer)
        s2[k] = (pg[k, 2 * c + 1 - yl] + r1[k, 1 - yl].astype(F32)).astype(BF16)
        wlink.send(2 + k, s2.at[k], r2.at[k], at.y_peer)
    sums = []
    for k in (0, 1):
        wlink.wait(2 + k, r2.at[k], at.y_peer)
        sums.append(pg[k, 2 * c + yl] + r1[k, yl].astype(F32) + r2[k].astype(F32))
    gate, up = sums
    mine = 2 * c + yl
    act[mine] = (gate / (1.0 + jnp.exp(-gate)) * up).astype(BF16)
    wlink.send(4, act.at[mine], act.at[mine], at.y_peer)
    wlink.send(5, act.at[mine], act.at[mine], at.core_peer)
    other = 2 * c + 1 - yl
    wlink.wait(4, act.at[other], at.y_peer)
    wlink.send(6, act.at[other], act.at[other], at.core_peer)
    wlink.wait(5, act.at[2 * (1 - c) + yl], at.core_peer)
    wlink.wait(6, act.at[2 * (1 - c) + 1 - yl], at.core_peer)
    wlink.finish()

    loads[3].wait()

    def down(i, _):
        cols = pl.ds(pl.multiple_of(i * step, step), step)
        rows = act[...].reshape(512, act.shape[2])
        acc[:, :, cols] = dot_nn(rows, wd[:, cols]).reshape(32, 16, step)
        return 0

    lax.fori_loop(0, width // step, down, 0)

    def emit_output(f, value):
        cols = pl.ds(f * half, half)
        out_ref[:, cols] = (res[:, cols].astype(F32) + value).astype(BF16)

    scatter(at, link, ylink, 3, acc, sbuf, rbuf, ysend, yrecv, emit_output)
    link.finish()
    ylink.finish()


VM = pl.BlockSpec(memory_space=pltpu.VMEM)
ANY = pl.BlockSpec(memory_space=pl.ANY)
DMA = pltpu.SemaphoreType.DMA


def qkv(hidden_in, gain, wq, wk, wv):
    width = hidden_in.shape[1]
    return pl.pallas_call(
        qkv_kernel,
        out_shape=jax.ShapeDtypeStruct((128, 384), BF16),
        in_specs=[VM, VM, ANY, ANY, ANY],
        out_specs=VM,
        scratch_shapes=[
            pltpu.VMEM((32, 16, width), BF16),
            pltpu.VMEM((width, 256), BF16),
            pltpu.VMEM((32, width), BF16),
            pltpu.VMEM((4, 128, 384), F32),
            pltpu.VMEM((4, 128, 384), BF16),
            pltpu.VMEM((3, 128, 384), BF16),
            pltpu.VMEM((16, 128), F32),
            pltpu.VMEM((3, 16, 128), F32),
            DMA((3,)),
            DMA((TREE,)), DMA((TREE,)),
            DMA((1,)), DMA((1,)),
            DMA((3,)), DMA((3,)),
            DMA((3,)), DMA((3,)),
        ],
        compiler_params=pltpu.CompilerParams(
            collective_id=0, has_side_effects=True, vmem_limit_bytes=40 * 2**20
        ),
    )(hidden_in, gain.reshape(1, -1), wq, wk.T, wv.T)


def mlp(att, hidden_in, gain, wo, wg, wu, wd):
    width = hidden_in.shape[1]
    units = wg.shape[1]
    return pl.pallas_call(
        mlp_kernel,
        out_shape=jax.ShapeDtypeStruct(hidden_in.shape, BF16),
        in_specs=[VM, VM, VM, ANY, ANY, ANY, ANY],
        out_specs=VM,
        scratch_shapes=[
            pltpu.VMEM((32, 16, width), BF16),
            pltpu.VMEM((256, width), BF16),
            pltpu.VMEM((units, width), BF16),
            pltpu.VMEM((units, width), BF16),
            pltpu.VMEM((units, width), BF16),
            pltpu.VMEM((32, 16, width), F32),
            pltpu.VMEM((TREE, 16, width // 2), BF16),
            pltpu.VMEM((TREE, 16, width // 2), BF16),
            pltpu.VMEM((2, 16, width // 2), BF16),
            pltpu.VMEM((2, 16, width // 2), BF16),
            pltpu.VMEM((16, width), BF16),
            pltpu.VMEM((16, 128), F32),
            pltpu.VMEM((3, 16, 128), F32),
            pltpu.VMEM((2, 4, 128, units), F32),
            pltpu.VMEM((2, 2, 128, units), BF16),
            pltpu.VMEM((2, 2, 128, units), BF16),
            pltpu.VMEM((2, 128, units), BF16),
            pltpu.VMEM((2, 128, units), BF16),
            pltpu.VMEM((4, 128, units), BF16),
            DMA((4,)),
            DMA((TREE,)), DMA((TREE,)),
            DMA((TREE,)), DMA((TREE,)),
            DMA((5,)), DMA((5,)),
            DMA((7,)), DMA((7,)),
            DMA((3,)), DMA((3,)),
        ],
        compiler_params=pltpu.CompilerParams(
            collective_id=1, has_side_effects=True, vmem_limit_bytes=60 * 2**20
        ),
    )(att, hidden_in, gain.reshape(1, -1), wo, wg.T, wu.T, wd)


def rotate(values, positions):
    half_size = values.shape[-1] // 2
    frequency = jnp.exp(
        jnp.arange(half_size, dtype=F32) * (-2.0 * math.log(rope_base) / values.shape[-1])
    )
    angles = positions.astype(F32)[:, None] * frequency[None, :]
    cosine = jnp.cos(angles)[:, None, :]
    sine_part = jnp.sin(angles)[:, None, :]
    first_half = values[..., :half_size]
    second_half = values[..., half_size:]
    return jnp.concatenate(
        [
            first_half * cosine - second_half * sine_part,
            second_half * cosine + first_half * sine_part,
        ],
        axis=-1,
    )


def attend(queries, key_fresh, value_fresh, key_cache, value_cache, lengths):
    row_count = queries.shape[0]
    group_size = HEADS // KV
    q_turned = rotate(queries.astype(F32), lengths).astype(BF16)
    k_turned = rotate(key_fresh.astype(F32), lengths).astype(BF16)
    grouped = q_turned.reshape(row_count, KV, group_size, HD)
    factor = HD ** (-0.5)
    scores = jnp.einsum("rghd,rjgd->rghj", grouped, key_cache, preferred_element_type=F32) * factor
    own_score = jnp.einsum("rghd,rgd->rgh", grouped, k_turned, preferred_element_type=F32) * factor
    slots = jnp.arange(key_cache.shape[1], dtype=jnp.int32)
    visible = slots[None, :] < lengths[:, None]
    scores = jnp.where(visible[:, None, None, :], scores, -jnp.inf)
    highest = jnp.maximum(jnp.max(scores, axis=-1), own_score)
    raised = jnp.exp(scores - highest[..., None])
    own_raised = jnp.exp(own_score - highest)
    totals = jnp.sum(raised, axis=-1) + own_raised
    weights = (raised / totals[..., None]).astype(BF16)
    own_weight = (own_raised / totals).astype(BF16)
    mixed = jnp.einsum("rghj,rjgd->rghd", weights, value_cache, preferred_element_type=F32)
    mixed = mixed + own_weight.astype(F32)[..., None] * value_fresh.astype(F32)[:, :, None, :]
    return mixed.reshape(row_count, HEADS * HD).astype(BF16)


def on_device(
    hidden_in,
    attn_gain,
    mlp_gain,
    w_query,
    w_key,
    w_value,
    w_out,
    w_gate,
    w_up,
    w_down,
    key_cache,
    value_cache,
    lengths,
):
    summed = qkv(hidden_in, attn_gain, w_query, w_key, w_value)[:, :288]
    spread = lax.all_to_all(summed, "hidden", split_axis=0, concat_axis=1, tiled=True)
    groups = lax.axis_size("hidden")
    row_count = spread.shape[0]
    pieces = spread.reshape(row_count, groups, -1)
    q_width = w_query.shape[1]
    k_width = w_key.shape[1]
    queries = pieces[:, :, :q_width].reshape(row_count, HEADS, HD)
    key_fresh = pieces[:, :, q_width : q_width + k_width].reshape(row_count, KV, HD)
    value_fresh = pieces[:, :, q_width + k_width :].reshape(row_count, KV, HD)
    attended = attend(queries, key_fresh, value_fresh, key_cache, value_cache, lengths)
    head_block = lax.all_to_all(attended, "hidden", split_axis=1, concat_axis=0, tiled=True)
    all_rows = lax.all_gather(head_block, "width", axis=0, tiled=True)
    return mlp(all_rows, hidden_in, mlp_gain, w_out, w_gate, w_up, w_down)


def solution(mesh):
    return jax.shard_map(
        on_device,
        mesh=mesh,
        in_specs=(
            P("hidden", "width"),
            P("width"),
            P("width"),
            P("width", "hidden"),
            P("width", "hidden"),
            P("width", "hidden"),
            P("hidden", "width"),
            P("width", "hidden"),
            P("width", "hidden"),
            P("hidden", "width"),
            P(("width", "hidden"), None, None, None),
            P(("width", "hidden"), None, None, None),
            P(("width", "hidden")),
        ),
        out_specs=P("hidden", "width"),
        check_vma=False,
    )
```

time: 731 us -> 247 us (0.34)
  waiting for transfers between devices: 624 us -> 17.7 us
  Pallas kernels: 0 us -> 199 us
  matrix products: 36.6 us -> 2.08 us
  blocking collectives: 31.9 us -> 6.42 us
  between operations: 13.7 us -> 0.14 us
  other arithmetic: 12.8 us -> 2.11 us
    reduce_scatter x3 -> x0, waiting for transfers between devices: 407 us -> none  [the longest x1 198 us: on_device(): lax.psum_scatter(jnp.dot(picked, w_out, preferred_element_type=jnp.float3...]
    pallas_call x0 -> x2, Pallas kernels: none -> 199 us  [the longest x1 153 us: mlp(): pl.pallas_call(mlp_kernel, out_shape=jax.ShapeDtypeStruct(hidden_in.shape...]
    all_gather x2 -> x0, waiting for transfers between devices: 158 us -> none  [the longest x1 82.5 us: on_device(): block_rows = lax.all_gather(normed, 'hidden', axis=0, tiled=True)]
    psum x1 -> x0, waiting for transfers between devices: 48.7 us -> none  [on_device(): lax.psum(both_parts.astype(jnp.bfloat16), 'width').astype(jnp.float32)]
    dot_general x8 -> x1, matrix products: 34.7 us -> 0.21 us  [attend(): jnp.einsum('rghd,rgd->rgh', grouped, k_turned, preferred_element_type=F32)]
    all_to_all x1 -> x0, blocking collectives: 13.4 us -> none  [on_device(): lax.all_to_all(attended, 'hidden', split_axis=1, concat_axis=0, tiled=True)]
    psum x2 -> x0, blocking collectives: 12.7 us -> none  [normalize(): totals = lax.psum(jnp.sum(widened * widened, axis=1), 'width')]
    all_to_all x0 -> x1, waiting for transfers between devices: none -> 9.21 us  [on_device(): lax.all_to_all(attended, 'hidden', split_axis=1, concat_axis=0, tiled=True)]
  transfers between devices with their start and end apart: 7 -> 2, of which waited for: 7 -> 2; matrix products, arithmetic and copies ran while one was open for 0% -> 1% of each run, Pallas kernels for 0% -> 0%
where the time goes in v1:
time: 247 us; the launch traced here: 246 us
  Pallas kernels  199 us (81%)
  waiting for transfers between devices  17.7 us (7%)
  starting transfers between devices  9.73 us (4%)
  local copies, waits for them, and re-layouts  8.86 us (4%)
  blocking collectives  6.42 us (3%)
    pallas_call x1, Pallas kernels, mlp(): pl.pallas_call(mlp_kernel, out_shape=jax.ShapeDtypeStruct(hidden_in.shape...  153 us
    pallas_call x1, Pallas kernels, qkv(): pl.pallas_call(qkv_kernel, out_shape=jax.ShapeDtypeStruct((128, 384), BF1...  46.3 us
    all_to_all x1, waiting for transfers between devices, on_device(): lax.all_to_all(attended, 'hidden', split_axis=1, concat_axis=0, tiled=True)  9.21 us
    all_to_all x1, waiting for transfers between devices, on_device(): lax.all_to_all(summed, 'hidden', split_axis=0, concat_axis=1, tiled=True)  8.47 us
    all_gather x1, blocking collectives, on_device(): all_rows = lax.all_gather(head_block, 'width', axis=0, tiled=True)  6.42 us
    all_to_all x1, starting transfers between devices, on_device(): lax.all_to_all(summed, 'hidden', split_axis=0, concat_axis=1, tiled=True)  5.88 us
    unnamed x13, local copies, waits for them, and re-layouts  5.87 us
  transfers between devices with their start and end apart: 2, of which 2 were waited for; matrix products, arithmetic and copies ran while one was open for 1% of the time, Pallas kernels for 0%

profile of v1, /device:TPU:0, one launch (start us, length us, event | category | flops | bytes accessed | tf_op | source)
XLA Modules:
  0.0 246.2 jit_solution(17394132244963786813)
XLA Ops:
  0.0 0.0 copy-start
  0.0 0.8 reshape.106.gain_ref
  0.8 0.0 copy-start.1
  0.8 1.6 copy-done.1
  2.4 0.9 copy-done.2
  3.3 0.9 copy-done.3
  4.2 0.9 copy-done.4
  5.1 46.3 %shard_map.127 = bf16[128,384]{1,0:T(8,128)(2,1)S(1)} custom-call(bf16[16,4096]{1,0:T(8,128)(2,1)S(1)} %copy-done.2, bf16[1,4096]{1,0:T(2,128)(2,1)S(1)} %reshape.106.gain_ref, bf16[4096,256]{1,0:T(8,128)(2,1)S(1)} %copy-done.1, bf16[16,4096]{1,0:T(8,128)(2,1)S(1)} %bitcast.18, bf16[16,4096]{1,0:T(8,128)(2,1)S(1)} %bitcast.19), custom_call_target="tpu_custom_call" | custom-call | tf_op jit(solution)/shard_map/pallas_call | solution.py:410
  51.4 0.7 all_to_all.24
  52.1 5.9 %all-to-all-start = ((bf16[32,4,288]{2,1,0:T(4,128)(2,1)}), bf16[32,4,288]{2,1,0:T(4,128)(2,1)S(1)}, u32[]{:S(2)}, u32[]{:S(2)}) async-start(bf16[32,4,288]{2,1,0:T(4,128)(2,1)} %all_to_all.24), calls=%async_computation | async-start | bytes 196608 | tf_op jit(solution)/shard_map/all_to_all | solution.py:535
  58.0 0.7 convert_element_type.47
  58.7 0.1 multiply_cosine_fusion
  58.8 0.7 iota_compare_fusion
  59.5 8.5 %all-to-all-done = bf16[32,4,288]{2,1,0:T(4,128)(2,1)S(1)} async-done(((bf16[32,4,288]{2,1,0:T(4,128)(2,1)}), bf16[32,4,288]{2,1,0:T(4,128)(2,1)S(1)}, u32[]{:S(2)}, u32[]{:S(2)}) %all-to-all-start) | async-done | bytes 73760 | tf_op jit(solution)/shard_map/all_to_all | solution.py:535
  68.0 0.1 slice_convert_fusion.2
  68.1 0.1 reshape.109
  68.2 0.1 subtract_convert_fusion
  68.3 0.1 subtract_convert_fusion.1
  68.4 0.1 maximum_bitcast_fusion
  68.5 0.2 fusion.7
  68.7 0.0 copy-done
  68.7 0.5 fusion.13
  69.2 0.2 fusion.4
  69.5 0.1 reshape.110
  69.6 1.4 fusion.1
  71.0 0.7 copy.30
  71.6 3.9 %all-to-all-start.1 = ((bf16[4,32,256]{2,0,1:T(4,128)(2,1)}), bf16[4,32,256]{2,0,1:T(4,128)(2,1)S(1)}, u32[]{:S(2)}, u32[]{:S(2)}) async-start(bf16[4,32,256]{2,0,1:T(4,128)(2,1)} %copy.30), calls=%async_computation.1 | async-start | bytes 131072 | tf_op jit(solution)/shard_map/all_to_all | solution.py:545
  75.5 0.6 reshape.107.gain_ref
  76.1 9.2 %all-to-all-done.1 = bf16[4,32,256]{2,0,1:T(4,128)(2,1)S(1)} async-done(((bf16[4,32,256]{2,0,1:T(4,128)(2,1)}), bf16[4,32,256]{2,0,1:T(4,128)(2,1)S(1)}, u32[]{:S(2)}, u32[]{:S(2)}) %all-to-all-start.1) | async-done | bytes 65568 | tf_op jit(solution)/shard_map/all_to_all | solution.py:545
  85.4 6.4 %all_gather.3.att_ref = bf16[512,256]{1,0:T(8,128)(2,1)} all-gather(bf16[128,256]{1,0:T(8,128)(2,1)S(1)} %all_to_all.29), channel_id=1, replica_groups=mesh['width'=4,'hidden'=32] {'width'}, dimensions={0}, use_global_device_ids=true | all-gather | bytes 327680 | tf_op jit(solution)/shard_map/all_gather | solution.py:546
  91.8 152.8 %shard_map.128 = bf16[16,4096]{1,0:T(8,128)(2,1)} custom-call(bf16[512,256]{1,0:T(8,128)(2,1)} %all_gather.3.att_ref, bf16[16,4096]{1,0:T(8,128)(2,1)} %hidden_ref.3, bf16[1,4096]{1,0:T(2,128)(2,1)} %reshape.107.gain_ref, bf16[256,4096]{1,0:T(8,128)(2,1)} %wo_hbm.1, bf16[832,4096]{1,0:T(8,128)(2,1)} %bitcast.20, bf16[832,4096]{1,0:T(8,128)(2,1)} %bitcast.21, ...), custom_call_target="tpu_custom_call" | custom-call | tf_op jit(solution)/shard_map/pallas_call | solution.py:439
  244.6 1.6 copy.44
  (13 shorter events, 0.1 us)
Async XLA Ops:
  0.0 68.7 %copy-start = (bf16[4,128,4,128]{3,2,1,0:T(4,128)(2,1)S(1)}, bf16[4,128,4,128]{3,2,1,0:T(4,128)(2,1)}, u32[]{:S(2)}) copy-start(bf16[4,128,4,128]{3,2,1,0:T(4,128)(2,1)} %param.23) | copy-start | bytes 1572868
  0.0 75.5 %copy-start.5 = (bf16[4096]{0:T(1024)(128)(2,1)S(1)}, bf16[4096]{0:T(1024)(128)(2,1)}, u32[]{:S(2)}) copy-start(bf16[4096]{0:T(1024)(128)(2,1)} %param.15) | copy-start | bytes 24580
  0.8 1.6 copy-start.1
  2.4 0.9 copy-start.2
  3.3 0.9 copy-start.3
  4.2 0.9 copy-start.4
  52.1 15.9 %all-to-all-start = ((bf16[32,4,288]{2,1,0:T(4,128)(2,1)}), bf16[32,4,288]{2,1,0:T(4,128)(2,1)S(1)}, u32[]{:S(2)}, u32[]{:S(2)}) async-start(bf16[32,4,288]{2,1,0:T(4,128)(2,1)} %all_to_all.24), calls=%async_computation | async-start | bytes 196608 | tf_op jit(solution)/shard_map/all_to_all | solution.py:535
  71.6 13.7 %all-to-all-start.1 = ((bf16[4,32,256]{2,0,1:T(4,128)(2,1)}), bf16[4,32,256]{2,0,1:T(4,128)(2,1)S(1)}, u32[]{:S(2)}, u32[]{:S(2)}) async-start(bf16[4,32,256]{2,0,1:T(4,128)(2,1)} %copy.30), calls=%async_computation.1 | async-start | bytes 131072 | tf_op jit(solution)/shard_map/all_to_all | solution.py:545

commit v2 on v1

v2 whole, which is shorter than its diff:
```python
import math

import jax
import jax.numpy as jnp
from jax import lax
from jax.experimental import pallas as pl
from jax.experimental.pallas import tpu as pltpu
from jax.sharding import PartitionSpec as P

D = 16384
HEADS = 64
KV = 4
HD = 128
MESH = pl.DeviceIdType.MESH
F32 = jnp.float32
BF16 = jnp.bfloat16

rope_base = 500000.0
norm_eps = 1e-05

OFFS = (0, -1, 1, 2)


class Place:
    def __init__(self):
        self.w = lax.axis_index("width")
        self.h = lax.axis_index("hidden")
        self.x = lax.rem(self.h, 4)
        self.z = lax.rem(self.h // 4, 4)
        self.yh = self.h // 16
        self.core = lax.rem(self.w, 2)
        self.yl = self.w // 2
        self.partner = (self.w, lax.rem(self.h + 16, 32))
        self.core_peer = (self.w + 1 - 2 * self.core, self.h)
        self.y_peer = (lax.rem(self.w + 2, 4), self.h)
        self.far_peer = (lax.rem(self.w + 2, 4) + 1 - 2 * self.core, self.h)

    def block(self, kind, f, p, q):
        dx, dz = (p, q) if f == 0 else (q, p)
        yh = self.yh if kind == 0 else 1 - self.yh
        return yh * 16 + lax.rem(self.z + (dz + 4), 4) * 4 + lax.rem(self.x + (dx + 4), 4)

    def neighbour(self, f, phase, sgn):
        if (f ^ phase) == 0:
            return (self.w, self.block(0, 0, sgn, 0))
        return (self.w, self.block(0, 0, 0, sgn))

    def along(self, i):
        return (self.w, lax.rem(self.h + i, 32))


def enter(at):
    barrier = pltpu.get_barrier_semaphore()
    peers = [at.core_peer, at.y_peer, at.far_peer] + [at.along(i) for i in range(1, 32)]
    for peer in peers:
        pl.semaphore_signal(barrier, inc=1, device_id=peer, device_id_type=MESH)
    pl.semaphore_wait(barrier, len(peers))


class Link:
    def __init__(self, ssem, rsem):
        self.ssem, self.rsem, self.sent = ssem, rsem, []

    def send(self, slot, src, dst, peer):
        copy = pltpu.make_async_remote_copy(
            src_ref=src,
            dst_ref=dst,
            send_sem=self.ssem.at[slot],
            recv_sem=self.rsem.at[slot],
            device_id=peer,
            device_id_type=MESH,
        )
        copy.start()
        self.sent.append(copy)

    def wait(self, slot, dst, peer):
        pltpu.make_async_remote_copy(
            src_ref=dst,
            dst_ref=dst,
            send_sem=self.ssem.at[slot],
            recv_sem=self.rsem.at[slot],
            device_id=peer,
            device_id_type=MESH,
        ).wait_recv()

    def finish(self):
        for copy in self.sent:
            copy.wait_send()
        self.sent = []


TREE = 60


def slot_of(kind, f, phase, j, d):
    base = (kind * 2 + f) * 15
    if phase == 0:
        return base + {1: 0, -1: 1, 0: 2}[d]
    return base + 3 + OFFS.index(j) * 3 + {1: 0, -1: 1, 0: 2}[d]


def gather_stages(at, link, g, kind, f):
    half = g.shape[2] // 2 // 128 * 128
    cols = pl.ds(0, half) if f == 0 else pl.ds(half, g.shape[2] - half)
    s = 1 if (kind ^ f) == 0 else -1

    def ref(p, q):
        return g.at[at.block(kind, f, p, q), :, cols]

    def send(phase, j, d, p, q, sgn):
        r = ref(p, q)
        link.send(slot_of(kind, f, phase, j, d), r, r, at.neighbour(f, phase, sgn))

    def wait(phase, j, d, p, q, sgn):
        link.wait(slot_of(kind, f, phase, j, d), ref(p, q), at.neighbour(f, phase, sgn))

    def spread(j):
        send(1, j, 1, j, 0, 1)
        send(1, j, -1, j, 0, -1)

    def relay(j):
        wait(1, j, s, j, -s, s)
        send(1, j, 0, j, -s, s)
        wait(1, j, -s, j, s, -s)

    send(0, 0, 1, 0, 0, 1)
    send(0, 0, -1, 0, 0, -1)
    spread(0)
    yield
    wait(0, 0, s, -s, 0, s)
    send(0, 0, 0, -s, 0, s)
    spread(-s)
    wait(0, 0, -s, s, 0, -s)
    spread(s)
    yield
    relay(0)
    wait(0, 0, 0, 2, 0, s)
    spread(2)
    yield
    relay(-s)
    relay(s)
    yield
    relay(2)
    yield
    for j in OFFS:
        wait(1, j, 0, j, 2, s)
    yield


def run(*groups):
    for gen in groups:
        next(gen)


def gather(at, link, ylink, yslot, g):
    mine = g.at[at.h]
    theirs = g.at[at.partner[1]]
    ylink.send(yslot, mine, mine, at.partner)
    o0, o1 = (gather_stages(at, link, g, 0, f) for f in (0, 1))
    p0, p1 = (gather_stages(at, link, g, 1, f) for f in (0, 1))
    run(o0, o1)
    yield
    run(o0, o1)
    ylink.wait(yslot, theirs, at.partner)
    run(p0, p1)
    run(o0, o1)
    run(p0, p1)
    run(o0, o1)
    run(p0, p1)
    run(o0, o1)
    run(p0, p1)
    run(o0, o1)
    yield
    run(p0, p1)
    yield
    run(p0, p1)
    yield


def scatter_stages(at, link, acc, sbuf, rbuf, kind, f, result):
    half = acc.shape[2] // 2
    s = 1 if (kind ^ f) == 0 else -1

    def own(p, q):
        return acc[at.block(kind, f, p, q), :, pl.ds(f * half, half)]

    def send(phase, j, d, sgn, value):
        slot = slot_of(kind, f, phase, j, d)
        sbuf[slot] = value.astype(BF16)
        link.send(slot, sbuf.at[slot], rbuf.at[slot], at.neighbour(f, phase, sgn))

    def take(phase, j, d, sgn):
        slot = slot_of(kind, f, phase, j, d)
        link.wait(slot, rbuf.at[slot], at.neighbour(f, phase, sgn))
        return rbuf[slot].astype(F32)

    def column(j):
        return own(j, 0) + take(1, j, s, s) + take(1, j, -s, -s)

    order = (2, -s, s, 0)
    for j in order:
        send(1, j, 0, s, own(j, 2))
    for j in order:
        send(1, j, -s, -s, own(j, -s))
    yield
    for j in order:
        send(1, j, s, s, own(j, s) + take(1, j, 0, s))
    yield
    send(0, 0, 0, s, column(2))
    send(0, 0, -s, -s, column(-s))
    yield
    send(0, 0, s, s, column(s) + take(0, 0, 0, s))
    yield
    result[f] = column(0) + take(0, 0, s, s) + take(0, 0, -s, -s)
    yield


def scatter(at, link, ylink, yslot, acc, sbuf, rbuf, ysend, yrecv, emit):
    far, near = {}, {}
    p0, p1 = (scatter_stages(at, link, acc, sbuf, rbuf, 1, f, far) for f in (0, 1))
    o0, o1 = (scatter_stages(at, link, acc, sbuf, rbuf, 0, f, near) for f in (0, 1))
    run(p0, p1)
    run(o0, o1)
    run(p0, p1)
    run(p0, p1)
    run(o0, o1)
    run(p0, p1)
    run(p0, p1)
    for f in (0, 1):
        ysend[f] = far[f].astype(BF16)
        ylink.send(yslot + f, ysend.at[f], yrecv.at[f], at.partner)
    run(o0, o1)
    run(o0, o1)
    run(o0, o1)
    for f in (0, 1):
        ylink.wait(yslot + f, yrecv.at[f], at.partner)
        emit(f, near[f] + yrecv[f].astype(F32))


def dot_nn(a, b):
    return jnp.dot(a, b, preferred_element_type=F32)


def dot_nt(a, b):
    return lax.dot_general(a, b, (((1,), (1,)), ((), ())), preferred_element_type=F32)


SS = 96


def split_sum(total, lanes, rest):
    high = total.astype(BF16).astype(F32)
    return jnp.where(lanes == SS, high, jnp.where(lanes == SS + 1, total - high, rest))


def joined_sum(tile, lanes):
    return jnp.sum(jnp.where((lanes == SS) | (lanes == SS + 1), tile, 0.0), axis=1, keepdims=True)


def lane_ids(rows):
    return lax.broadcasted_iota(jnp.int32, (rows, 128), 1)


def fill_own(at, g, values, gain):
    width = values.shape[1]
    part = jnp.sum(values * values, axis=1, keepdims=True)
    g[at.h, :, pl.ds(0, width)] = (values * gain).astype(BF16)
    lanes = lane_ids(values.shape[0])
    g[at.h, :, pl.ds(width, 128)] = split_sum(part, lanes, jnp.zeros(lanes.shape, F32)).astype(BF16)


def exchange(at, link, src, dst):
    for i in range(1, 32):
        peer = at.along(i)
        link.send(i, src(peer[1]), dst(at.h), peer)


def exchanged(at, link, dst):
    for i in range(1, 32):
        peer = at.along(32 - i)
        link.wait(i, dst(peer[1]), peer)


def turn(values, cosine, sine):
    return values * cosine + pltpu.roll(values, HD // 2, 1) * sine


def attend(lengths, rqf, kc, vc, out):
    pairs = HEADS // 2
    lane = lax.broadcasted_iota(jnp.int32, (1, HD), 1)
    entry = lax.rem(lane, HD // 2).astype(F32)
    frequency = jnp.exp(entry * (-2.0 * math.log(rope_base) / HD))
    count = kc.shape[1]
    place = lax.broadcasted_iota(jnp.int32, (HEADS, count), 1)
    head_group = lax.rem(lax.broadcasted_iota(jnp.int32, (HEADS, count), 0), pairs) // (pairs // KV)
    same_group = lax.rem(place, KV) == head_group
    slot = place // KV
    factor = HD ** (-0.5)

    def widen(fresh):
        each = jnp.broadcast_to(fresh[:, None, :], (KV, pairs // KV, HD)).reshape(pairs, HD)
        return jnp.concatenate([each, each], axis=0)

    for r in range(4):
        def piece(t):
            return rqf[pl.ds(4 * t + r, pairs, stride=16), :]

        position = lengths[r]
        angle = frequency * position.astype(F32)
        cosine = jnp.cos(angle)
        sine = jnp.where(lane < HD // 2, -1.0, 1.0) * jnp.sin(angle)
        q = turn(jnp.concatenate([piece(0), piece(1)], axis=0), cosine, sine).astype(BF16)
        k_fresh = jnp.sum(piece(2).reshape(KV, pairs // KV, HD), axis=1)
        v_fresh = jnp.sum(piece(3).reshape(KV, pairs // KV, HD), axis=1)
        k_turned = turn(k_fresh, cosine, sine).astype(BF16).astype(F32)
        own = jnp.sum(q.astype(F32) * widen(k_turned), axis=1, keepdims=True) * factor
        visible = same_group & (slot < position)
        scores = jnp.where(visible, dot_nt(q, kc[r]) * factor, -jnp.inf)
        highest = jnp.maximum(jnp.max(scores, axis=1, keepdims=True), own)
        raised = jnp.exp(scores - highest)
        own_raised = jnp.exp(own - highest)
        total = jnp.sum(raised, axis=1, keepdims=True) + own_raised
        weights = (raised / total).astype(BF16)
        own_weight = (own_raised / total).astype(BF16).astype(F32)
        mixed = dot_nn(weights, vc[r]) + own_weight * widen(v_fresh)
        mixed = mixed.astype(BF16).astype(F32)
        for t in (0, 1):
            out[pl.ds(4 * t + r, pairs, stride=8), :] = mixed[t * pairs : (t + 1) * pairs]


def layer_kernel(
    hidden_ref, gains_ref, lengths, wq_hbm, wk_hbm, wv_hbm, wo_hbm, wg_hbm, wu_hbm, wd_hbm, kc_hbm, vc_hbm,
    out_ref,
    g, wq, wkv, wo, wgu, wd, kc, vc, acc, sbuf, rbuf, ysend, yrecv, res,
    qkv, qkv_s, qkv_r, heads, msgf, msg, rq, rqf, msg2, rq2, attf, att,
    pg, s1, r1, s2, r2, act,
    lsem, gss, grs, ssem, rsem, yss, yrs, wss, wrs, ass, ars, bss, brs,
):
    at = Place()
    width = hidden_ref.shape[1]
    units = wd.shape[0]
    half = width // 2
    loads = [
        pltpu.make_async_copy(src, dst, lsem.at[i])
        for i, (src, dst) in enumerate(
            (
                (wq_hbm, wq),
                (wk_hbm, wkv.at[pl.ds(0, 16)]),
                (wv_hbm, wkv.at[pl.ds(16, 16)]),
                (kc_hbm, kc),
                (vc_hbm, vc),
                (wo_hbm, wo),
                (wg_hbm, wgu.at[0, pl.ds(0, units)]),
                (wu_hbm, wgu.at[1, pl.ds(0, units)]),
                (wd_hbm, wd),
            )
        )
    ]
    for load in loads:
        load.start()
    fill_own(at, g, hidden_ref[...].astype(F32), gains_ref[0:1, :].astype(F32))
    enter(at)
    glink, link, ylink = Link(gss, grs), Link(ssem, rsem), Link(yss, yrs)
    wlink, alink, blink = Link(wss, wrs), Link(ass, ars), Link(bss, brs)
    mates = (at.core_peer, at.y_peer, at.far_peer)

    first = gather(at, glink, ylink, 0, g)
    next(first)
    wkv[pl.ds(32, 96), :] = jnp.zeros((96, width), BF16)
    for k in (0, 1):
        wgu[k, pl.ds(units, 64), :] = jnp.zeros((64, width), BF16)
    for load in loads[:3]:
        load.wait()
    for _ in first:
        pass
    glink.finish()
    ylink.finish()
    for i in range(4):
        rows = g[pl.ds(i * 8, 8), :, pl.ds(0, width)].reshape(128, width)
        tail = g[pl.ds(i * 8, 8), :, pl.ds(width, 128)].reshape(128, 128).astype(F32)
        qkv[i, :, pl.ds(0, 256)] = dot_nn(rows, wq[...])
        qkv[i, :, pl.ds(256, 128)] = dot_nt(rows, wkv[...]) + tail
    qkv_s[...] = qkv[...].astype(BF16)
    for i, peer in enumerate(mates):
        wlink.send(i, qkv_s.at[peer[0]], qkv_r.at[i], peer)
    total = qkv[at.w]
    for i, peer in enumerate(mates):
        wlink.wait(i, qkv_r.at[i], peer)
        total = total + qkv_r[i].astype(F32)
    norm = lax.rsqrt(joined_sum(total[:, 256:], lane_ids(128)) / D + norm_eps)
    scaled = (total * norm).astype(BF16)
    row = lax.broadcasted_iota(jnp.int32, (128, 256), 0)
    col = lax.broadcasted_iota(jnp.int32, (128, 256), 1)
    wanted = 16 * (col // 128) + lax.rem(col, 16)
    placed = (row == wanted) & (lax.rem(col, 128) // 16 == lax.rem(at.h, 8))
    fresh = dot_nn(scaled[:, 256:], jnp.where(placed, 1.0, 0.0).astype(BF16))
    heads[0] = scaled[:, :128].astype(F32)
    heads[1] = scaled[:, 128:256].astype(F32)
    heads[2] = fresh[:, :128]
    heads[3] = fresh[:, 128:]
    for t in range(4):
        for r in range(4):
            msgf[pl.ds(4 * t + r, 32, stride=16), :] = heads[t, pl.ds(r, 32, stride=4), :]
    msg[...] = msgf[...].astype(BF16).reshape(32, 16, 128)
    exchange(at, alink, lambda d: msg.at[d], lambda d: rq.at[d])
    rq[at.h] = msg[at.h]
    loads[3].wait()
    loads[4].wait()
    exchanged(at, alink, lambda d: rq.at[d])
    rqf[...] = rq[...].astype(F32).reshape(512, 128)
    attend(lengths, rqf, kc, vc, msg2)

    def eight(ref):
        return lambda d: ref.at[pl.ds(pl.multiple_of(d * 8, 8), 8)]

    exchange(at, blink, eight(msg2), eight(rq2))
    own8 = pl.ds(pl.multiple_of(at.h * 8, 8), 8)
    rq2[own8, :] = msg2[own8, :]
    exchanged(at, blink, eight(rq2))
    for t in (0, 1):
        for r in range(4):
            attf[t, pl.ds(r, 32, stride=4), :] = rq2[pl.ds(4 * t + r, 32, stride=8), :]
        att[at.w, :, pl.ds(t * 128, 128)] = attf[t].astype(BF16)
    for i, peer in enumerate(mates):
        wlink.send(3 + i, att.at[at.w], att.at[at.w], peer)
    loads[5].wait()
    for i, peer in enumerate(mates):
        wlink.wait(3 + i, att.at[peer[0]], peer)
    wlink.finish()
    alink.finish()
    blink.finish()
    for i in range(4):
        cols = pl.ds(i * 1024, 1024)
        acc[:, :, cols] = dot_nn(att[...].reshape(512, 256), wo[:, cols]).reshape(32, 16, 1024)

    def emit_residual(f, value):
        cols = pl.ds(f * half, half)
        res[:, cols] = (hidden_ref[:, cols].astype(F32) + value).astype(BF16)

    scatter(at, link, ylink, 1, acc, sbuf, rbuf, ysend, yrecv, emit_residual)
    link.finish()
    ylink.finish()

    fill_own(at, g, res[...].astype(F32), gains_ref[1:2, :].astype(F32))
    for load in loads[6:]:
        load.wait()
    c, yl = at.core, at.yl
    planes = (at.yh, 1 - at.yh)

    def plane(kind):
        return pl.ds(pl.multiple_of(planes[kind] * 16, 16), 16)

    def gate_up(kind, k):
        rows = g[plane(kind), :, pl.ds(0, width)].reshape(256, width)
        for start, size in ((0, 256), (256, 256), (512, 384)):
            value = dot_nt(rows, wgu[k, pl.ds(start, size), :])
            pg[k, kind, :, :, pl.ds(start, size)] = value.reshape(4, 64, size)
        if k == 0:
            tail = g[plane(kind), :, pl.ds(width, 128)].reshape(4, 64, 128).astype(F32)
            last = pl.ds(768, 128)
            pg[0, kind, :, :, last] = pg[0, kind, :, :, last] + tail
        s1[kind, k] = pg[k, kind, pl.ds(2 * (1 - c), 2)].astype(BF16)
        wlink.send(6 + kind * 7 + k, s1.at[kind, k], r1.at[kind, k], at.core_peer)

    def over_y(kind):
        for k in (0, 1):
            slot = 6 + kind * 7 + k
            wlink.wait(slot, r1.at[kind, k], at.core_peer)
            value = pg[k, kind, 2 * c + 1 - yl] + r1[kind, k, 1 - yl].astype(F32)
            s2[kind, k] = value.astype(BF16)
            if k == 0:
                lanes = lane_ids(64)
                tile = value[:, 768:]
                s2[kind, k, :, pl.ds(768, 128)] = split_sum(joined_sum(tile, lanes), lanes, tile).astype(BF16)
            wlink.send(slot + 2, s2.at[kind, k], r2.at[kind, k], at.y_peer)

    def activate(kind):
        base = 6 + kind * 7
        sums = []
        for k in (0, 1):
            wlink.wait(base + 2 + k, r2.at[kind, k], at.y_peer)
            sums.append(
                pg[k, kind, 2 * c + yl] + r1[kind, k, yl].astype(F32) + r2[kind, k].astype(F32)
            )
        scale = lax.rsqrt(joined_sum(sums[0][:, 768:], lane_ids(64)) / D + norm_eps)
        gate, up = sums[0][:, :units] * scale, sums[1][:, :units] * scale
        mine = act.at[kind, 2 * c + yl]
        act[kind, 2 * c + yl] = (gate / (1.0 + jnp.exp(-gate)) * up).astype(BF16)
        wlink.send(base + 4, mine, mine, at.y_peer)
        wlink.send(base + 5, mine, mine, at.core_peer)

    def pass_on(kind):
        base = 6 + kind * 7
        other = act.at[kind, 2 * c + 1 - yl]
        wlink.wait(base + 4, other, at.y_peer)
        wlink.send(base + 6, other, other, at.core_peer)

    def complete(kind):
        base = 6 + kind * 7
        wlink.wait(base + 5, act.at[kind, 2 * (1 - c) + yl], at.core_peer)
        wlink.wait(base + 6, act.at[kind, 2 * (1 - c) + 1 - yl], at.core_peer)

    def down(kind):
        rows = act[kind].reshape(256, units)
        for i in range(4):
            cols = pl.ds(i * 1024, 1024)
            acc[plane(kind), :, cols] = dot_nn(rows, wd[:, cols]).reshape(16, 16, 1024)

    near, far = {}, {}
    o0, o1 = (scatter_stages(at, link, acc, sbuf, rbuf, 0, f, near) for f in (0, 1))
    p0, p1 = (scatter_stages(at, link, acc, sbuf, rbuf, 1, f, far) for f in (0, 1))

    second = gather(at, glink, ylink, 3, g)
    next(second)
    next(second)
    gate_up(0, 0)
    next(second)
    gate_up(0, 1)
    over_y(0)
    next(second)
    gate_up(1, 0)
    activate(0)
    gate_up(1, 1)
    pass_on(0)
    over_y(1)
    complete(0)
    down(0)
    run(o0, o1)
    activate(1)
    run(o0, o1)
    pass_on(1)
    complete(1)
    down(1)
    run(p0, p1)
    run(o0, o1)
    run(p0, p1)
    run(o0, o1)
    run(p0, p1)
    run(o0, o1)
    run(p0, p1)
    run(p0, p1)
    for f in (0, 1):
        ysend[f] = far[f].astype(BF16)
        ylink.send(4 + f, ysend.at[f], yrecv.at[f], at.partner)
    for f in (0, 1):
        cols = pl.ds(f * half, half)
        ylink.wait(4 + f, yrecv.at[f], at.partner)
        value = res[:, cols].astype(F32) + near[f] + yrecv[f].astype(F32)
        out_ref[:, cols] = value.astype(BF16)
    for each in (glink, link, ylink, wlink):
        each.finish()


VM = pl.BlockSpec(memory_space=pltpu.VMEM)
ANY = pl.BlockSpec(memory_space=pl.ANY)
DMA = pltpu.SemaphoreType.DMA


def on_device(
    hidden_in,
    attn_gain,
    mlp_gain,
    w_query,
    w_key,
    w_value,
    w_out,
    w_gate,
    w_up,
    w_down,
    key_cache,
    value_cache,
    lengths,
):
    width = hidden_in.shape[1]
    units = w_gate.shape[1]
    padded = units + 64
    slots = key_cache.shape[1] * KV
    return pl.pallas_call(
        layer_kernel,
        out_shape=jax.ShapeDtypeStruct(hidden_in.shape, BF16),
        in_specs=[VM, VM, pl.BlockSpec(memory_space=pltpu.SMEM)] + [ANY] * 9,
        out_specs=VM,
        scratch_shapes=[
            pltpu.VMEM((32, 16, width + 128), BF16),
            pltpu.VMEM((width, 256), BF16),
            pltpu.VMEM((128, width), BF16),
            pltpu.VMEM((256, width), BF16),
            pltpu.VMEM((2, padded, width), BF16),
            pltpu.VMEM((units, width), BF16),
            pltpu.VMEM((4, slots, HD), BF16),
            pltpu.VMEM((4, slots, HD), BF16),
            pltpu.VMEM((32, 16, width), F32),
            pltpu.VMEM((TREE, 16, width // 2), BF16),
            pltpu.VMEM((TREE, 16, width // 2), BF16),
            pltpu.VMEM((2, 16, width // 2), BF16),
            pltpu.VMEM((2, 16, width // 2), BF16),
            pltpu.VMEM((16, width), BF16),
            pltpu.VMEM((4, 128, 384), F32),
            pltpu.VMEM((4, 128, 384), BF16),
            pltpu.VMEM((3, 128, 384), BF16),
            pltpu.VMEM((4, 128, 128), F32),
            pltpu.VMEM((512, 128), F32),
            pltpu.VMEM((32, 16, 128), BF16),
            pltpu.VMEM((32, 16, 128), BF16),
            pltpu.VMEM((512, 128), F32),
            pltpu.VMEM((256, 128), F32),
            pltpu.VMEM((256, 128), F32),
            pltpu.VMEM((2, 128, 128), F32),
            pltpu.VMEM((4, 128, 256), BF16),
            pltpu.VMEM((2, 2, 4, 64, padded), F32),
            pltpu.VMEM((2, 2, 2, 64, padded), BF16),
            pltpu.VMEM((2, 2, 2, 64, padded), BF16),
            pltpu.VMEM((2, 2, 64, padded), BF16),
            pltpu.VMEM((2, 2, 64, padded), BF16),
            pltpu.VMEM((2, 4, 64, units), BF16),
            DMA((9,)),
            DMA((TREE,)), DMA((TREE,)),
            DMA((TREE,)), DMA((TREE,)),
            DMA((6,)), DMA((6,)),
            DMA((20,)), DMA((20,)),
            DMA((32,)), DMA((32,)),
            DMA((32,)), DMA((32,)),
        ],
        compiler_params=pltpu.CompilerParams(
            collective_id=0, has_side_effects=True, vmem_limit_bytes=63 * 2**20
        ),
    )(
        hidden_in,
        jnp.stack([attn_gain, mlp_gain]),
        lengths,
        w_query,
        w_key.T,
        w_value.T,
        w_out,
        w_gate.T,
        w_up.T,
        w_down,
        key_cache.reshape(4, slots, HD),
        value_cache.reshape(4, slots, HD),
    )


def solution(mesh):
    return jax.shard_map(
        on_device,
        mesh=mesh,
        in_specs=(
            P("hidden", "width"),
            P("width"),
            P("width"),
            P("width", "hidden"),
            P("width", "hidden"),
            P("width", "hidden"),
            P("hidden", "width"),
            P("width", "hidden"),
            P("width", "hidden"),
            P("hidden", "width"),
            P(("width", "hidden"), None, None, None),
            P(("width", "hidden"), None, None, None),
            P(("width", "hidden")),
        ),
        out_specs=P("hidden", "width"),
        check_vma=False,
    )
```

time: 247 us -> 189 us (0.77)
  waiting for transfers between devices: 17.7 us -> 0 us
  Pallas kernels: 199 us -> 185 us
  starting transfers between devices: 9.73 us -> 0 us
  blocking collectives: 6.42 us -> 0 us
  local copies, waits for them, and re-layouts: 8.86 us -> 2.99 us
    all_to_all x2 -> x0, waiting for transfers between devices: 17.7 us -> none  [the longest x1 9.21 us: on_device(): lax.all_to_all(attended, 'hidden', split_axis=1, concat_axis=0, tiled=True)]
    pallas_call x2 -> x1, Pallas kernels: 199 us -> 185 us  [on_device(): pl.pallas_call(layer_kernel, out_shape=jax.ShapeDtypeStruct(hidden_in.sha...]
    all_to_all x2 -> x0, starting transfers between devices: 9.73 us -> none  [the longest x1 5.88 us: on_device(): lax.all_to_all(summed, 'hidden', split_axis=0, concat_axis=1, tiled=True)]
    all_gather x1 -> x0, blocking collectives: 6.42 us -> none  [on_device(): all_rows = lax.all_gather(head_block, 'width', axis=0, tiled=True)]
    unnamed x13 -> x1, local copies, waits for them, and re-layouts: 5.87 us -> 1.57 us
  transfers between devices with their start and end apart: 2 -> 0, of which waited for: 2 -> 0; matrix products, arithmetic and copies ran while one was open for 1% -> 0% of each run, Pallas kernels for 0% -> 0%
where the time goes in v2:
time: 189 us
  Pallas kernels  185 us (98%)
  local copies, waits for them, and re-layouts  2.99 us (2%)
    pallas_call x1, Pallas kernels, on_device(): pl.pallas_call(layer_kernel, out_shape=jax.ShapeDtypeStruct(hidden_in.sha...  185 us

profile of v2, /device:TPU:0, one launch (start us, length us, event | category | flops | bytes accessed | tf_op | source)
XLA Modules:
  0.0 188.6 jit_solution(13503058081840766269)
XLA Ops:
  0.0 0.7 stack.9
  0.7 0.7 stack.10
  1.4 0.6 pad_maximum_fusion.gains_ref
  2.1 185.0 %shard_map.127 = bf16[16,4096]{1,0:T(8,128)(2,1)} custom-call(bf16[16,4096]{1,0:T(8,128)(2,1)} %hidden_ref.1, bf16[2,4096]{1,0:T(2,128)(2,1)} %pad_maximum_fusion.gains_ref, s32[4]{0:T(128)} %lengths.1, bf16[4096,256]{1,0:T(8,128)(2,1)} %wq_hbm.1, bf16[16,4096]{1,0:T(8,128)(2,1)} %bitcast.10, bf16[16,4096]{1,0:T(8,128)(2,1)} %bitcast.11, ...), custom_call_target="tpu_custom_call" | custom-call | tf_op jit(solution)/shard_map/pallas_call | solution.py:578
  187.1 1.6 copy.15

commit v3 on v0

v3 whole, which is shorter than its diff:
```python
import functools
import math

import jax
import jax.numpy as jnp
from jax import lax
from jax.experimental import pallas as pl
from jax.experimental.pallas import tpu as pltpu
from jax.sharding import PartitionSpec as P

D = 16384
HEADS = 64
KV = 4
HD = 128
MESH = pl.DeviceIdType.MESH
F32 = jnp.float32
BF16 = jnp.bfloat16

rope_base = 500000.0
norm_eps = 1e-05

OFFS = (0, -1, 1, 2)


class Place:
    def __init__(self):
        self.w = lax.axis_index("width")
        self.h = lax.axis_index("hidden")
        self.x = lax.rem(self.h, 4)
        self.z = lax.rem(self.h // 4, 4)
        self.yh = self.h // 16
        self.core = lax.rem(self.w, 2)
        self.yl = self.w // 2
        self.partner = (self.w, lax.rem(self.h + 16, 32))
        self.core_peer = (self.w + 1 - 2 * self.core, self.h)
        self.y_peer = (lax.rem(self.w + 2, 4), self.h)
        self.far_peer = (lax.rem(self.w + 2, 4) + 1 - 2 * self.core, self.h)

    def block(self, c, f, p, q):
        dx, dz = (p, q) if f == 0 else (q, p)
        return c * 16 + lax.rem(self.z + (dz + 4), 4) * 4 + lax.rem(self.x + (dx + 4), 4)

    def neighbour(self, f, phase, sgn):
        p, q = (sgn, 0) if phase == 0 else (0, sgn)
        return (self.w, self.yh * 16 + self.block(0, f, p, q))

    def along(self, i):
        return (self.w, lax.rem(self.h + i, 32))


def enter(at):
    barrier = pltpu.get_barrier_semaphore()
    peers = [at.core_peer, at.y_peer, at.far_peer] + [at.along(i) for i in range(1, 32)]
    for peer in peers:
        pl.semaphore_signal(barrier, inc=1, device_id=peer, device_id_type=MESH)
    pl.semaphore_wait(barrier, len(peers))


class Link:
    def __init__(self, ssem, rsem, peer):
        self.ssem, self.rsem, self.peer, self.sent = ssem, rsem, peer, {}

    def copy(self, slot, src, dst, peer):
        return pltpu.make_async_remote_copy(
            src_ref=src,
            dst_ref=dst,
            send_sem=self.ssem.at[slot],
            recv_sem=self.rsem.at[slot],
            device_id=peer,
            device_id_type=MESH,
        )

    def send(self, slot, src, dst, peer, key=None, like=None):
        self.copy(slot, src, dst, peer).start()
        self.sent[(slot, key)] = like or (lambda: src)

    def wait(self, slot, dst, peer):
        self.copy(slot, dst, dst, peer).wait_recv()

    def finish(self, slots=None, key=None):
        for which in [w for w in self.sent if w[1] == key and (slots is None or w[0] in slots)]:
            like = self.sent.pop(which)()
            self.copy(which[0], like, like, self.peer).wait_send()


def only(flag, body):
    pl.when(flag[0] == flag[1])(body)


TREE = 60


def slots_of(c, f):
    return range((c * 2 + f) * 15, (c * 2 + f) * 15 + 15)


def slot_of(c, f, phase, j, d):
    base = (c * 2 + f) * 15
    if phase == 0:
        return base + {1: 0, -1: 1, 0: 2}[d]
    return base + 3 + OFFS.index(j) * 3 + {1: 0, -1: 1, 0: 2}[d]


class Gather:
    def __init__(self, at, link, g, c, f):
        half = g.shape[2] // 2 // 128 * 128
        self.cols = pl.ds(0, half) if f == 0 else pl.ds(half, g.shape[2] - half)
        self.at, self.link, self.g, self.c, self.f = at, link, g, c, f
        self.s = 1 if (c ^ f) == 0 else -1

    def ref(self, p, q):
        return self.g.at[self.at.block(self.c, self.f, p, q), :, self.cols]

    def send(self, phase, j, d, p, q, sgn):
        r = self.ref(p, q)
        slot = slot_of(self.c, self.f, phase, j, d)
        self.link.send(slot, r, r, self.at.neighbour(self.f, phase, sgn))

    def wait(self, phase, j, d, p, q, sgn):
        slot = slot_of(self.c, self.f, phase, j, d)
        self.link.wait(slot, self.ref(p, q), self.at.neighbour(self.f, phase, sgn))

    def spread(self, j):
        self.send(1, j, self.s, j, 0, self.s)
        self.send(1, j, -self.s, j, 0, -self.s)

    def start(self):
        self.send(0, 0, self.s, 0, 0, self.s)
        self.send(0, 0, -self.s, 0, 0, -self.s)
        self.spread(0)

    def first(self):
        s = self.s
        self.wait(0, 0, s, -s, 0, s)
        self.send(0, 0, 0, -s, 0, s)
        self.spread(-s)

    def second(self):
        s = self.s
        self.wait(0, 0, -s, s, 0, -s)
        self.spread(s)

    def third(self):
        self.wait(0, 0, 0, 2, 0, self.s)
        self.spread(2)

    def relay(self, j):
        s = self.s
        self.wait(1, j, s, j, -s, s)
        self.send(1, j, 0, j, -s, s)

    def end(self):
        for j in OFFS:
            self.wait(1, j, -self.s, j, self.s, -self.s)
        for j in OFFS:
            self.wait(1, j, 0, j, 2, self.s)

    def tasks(self, add, name):
        add(f"{name}.start", self.start)
        add(f"{name}.first", self.first)
        add(f"{name}.second", self.second)
        add(f"{name}.third", self.third)
        for j in (0, -self.s, self.s, 2):
            add(f"{name}.relay{j}", functools.partial(self.relay, j))


class Scatter:
    def __init__(self, at, link, acc, sbuf, rbuf, c, f):
        half = acc.shape[2] // 2
        self.cols = pl.ds(f * half, half)
        self.at, self.link, self.acc, self.sbuf, self.rbuf, self.c, self.f = at, link, acc, sbuf, rbuf, c, f
        self.s = 1 if (c ^ f) == 0 else -1

    def own(self, p, q):
        return self.acc[self.at.block(self.c, self.f, p, q), :, self.cols]

    def send(self, phase, j, d, sgn, value):
        slot = slot_of(self.c, self.f, phase, j, d)
        self.sbuf[slot] = value.astype(BF16)
        self.link.send(slot, self.sbuf.at[slot], self.rbuf.at[slot], self.at.neighbour(self.f, phase, sgn))

    def take(self, phase, j, d, sgn):
        slot = slot_of(self.c, self.f, phase, j, d)
        self.link.wait(slot, self.rbuf.at[slot], self.at.neighbour(self.f, phase, sgn))
        return self.rbuf[slot].astype(F32)

    def column(self, j):
        s = self.s
        return self.own(j, 0) + self.take(1, j, s, s) + self.take(1, j, -s, -s)

    def far(self, j):
        self.send(1, j, 0, self.s, self.own(j, 2))

    def back(self, j):
        self.send(1, j, -self.s, -self.s, self.own(j, -self.s))

    def on(self, j):
        self.send(1, j, self.s, self.s, self.own(j, self.s) + self.take(1, j, 0, self.s))

    def line_far(self):
        self.send(0, 0, 0, self.s, self.column(2))

    def line_back(self):
        self.send(0, 0, -self.s, -self.s, self.column(-self.s))

    def line_on(self):
        self.send(0, 0, self.s, self.s, self.column(self.s) + self.take(0, 0, 0, self.s))

    def total(self):
        return self.column(0) + self.take(0, 0, self.s, self.s) + self.take(0, 0, -self.s, -self.s)

    def tasks(self, add, name):
        order = (2, -self.s, self.s, 0)
        for j in order:
            add(f"{name}.far{j}", functools.partial(self.far, j), 0.06)
        for j in order:
            add(f"{name}.back{j}", functools.partial(self.back, j), 0.06)
        for j in order:
            add(f"{name}.on{j}", functools.partial(self.on, j), 0.08)
        add(f"{name}.line_far", self.line_far, 0.1)
        add(f"{name}.line_back", self.line_back, 0.1)
        add(f"{name}.line_on", self.line_on, 0.1)


def dot_nn(a, b):
    return jnp.dot(a, b, preferred_element_type=F32)


def dot_nt(a, b):
    return lax.dot_general(a, b, (((1,), (1,)), ((), ())), preferred_element_type=F32)


SS = 96


def split_sum(total, lanes, rest):
    high = total.astype(BF16).astype(F32)
    return jnp.where(lanes == SS, high, jnp.where(lanes == SS + 1, total - high, rest))


def joined_sum(tile, lanes):
    return jnp.sum(jnp.where((lanes == SS) | (lanes == SS + 1), tile, 0.0), axis=1, keepdims=True)


def lane_ids(rows):
    return lax.broadcasted_iota(jnp.int32, (rows, 128), 1)


def fill_own(at, g, values, gain):
    width = values.shape[1]
    part = jnp.sum(values * values, axis=1, keepdims=True)
    g[at.h, :, pl.ds(0, width)] = (values * gain).astype(BF16)
    lanes = lane_ids(values.shape[0])
    g[at.h, :, pl.ds(width, 128)] = split_sum(part, lanes, jnp.zeros(lanes.shape, F32)).astype(BF16)


def exchange(at, link, src, dst, key, like):
    for i in range(1, 32):
        peer = at.along(i)
        link.send(i, src(peer[1]), dst(at.h), peer, key, like)


def exchanged(at, link, dst):
    for i in range(1, 32):
        peer = at.along(32 - i)
        link.wait(i, dst(peer[1]), peer)


def turn(values, cosine, sine):
    return values * cosine + pltpu.roll(values, HD // 2, 1) * sine


def attend(lengths, rqf, kc, vc, out):
    pairs = HEADS // 2
    lane = lax.broadcasted_iota(jnp.int32, (1, HD), 1)
    entry = lax.rem(lane, HD // 2).astype(F32)
    frequency = jnp.exp(entry * (-2.0 * math.log(rope_base) / HD))
    count = kc.shape[1]
    place = lax.broadcasted_iota(jnp.int32, (HEADS, count), 1)
    head_group = lax.rem(lax.broadcasted_iota(jnp.int32, (HEADS, count), 0), pairs) // (pairs // KV)
    same_group = lax.rem(place, KV) == head_group
    slot = place // KV
    factor = HD ** (-0.5)

    def widen(fresh):
        each = jnp.broadcast_to(fresh[:, None, :], (KV, pairs // KV, HD)).reshape(pairs, HD)
        return jnp.concatenate([each, each], axis=0)

    for r in range(4):
        def piece(t):
            return rqf[pl.ds(4 * t + r, pairs, stride=16), :]

        position = lengths[r]
        angle = frequency * position.astype(F32)
        cosine = jnp.cos(angle)
        sine = jnp.where(lane < HD // 2, -1.0, 1.0) * jnp.sin(angle)
        q = turn(jnp.concatenate([piece(0), piece(1)], axis=0), cosine, sine).astype(BF16)
        k_fresh = jnp.sum(piece(2).reshape(KV, pairs // KV, HD), axis=1)
        v_fresh = jnp.sum(piece(3).reshape(KV, pairs // KV, HD), axis=1)
        k_turned = turn(k_fresh, cosine, sine).astype(BF16).astype(F32)
        own = jnp.sum(q.astype(F32) * widen(k_turned), axis=1, keepdims=True) * factor
        visible = same_group & (slot < position)
        scores = jnp.where(visible, dot_nt(q, kc[r]) * factor, -jnp.inf)
        highest = jnp.maximum(jnp.max(scores, axis=1, keepdims=True), own)
        raised = jnp.exp(scores - highest)
        own_raised = jnp.exp(own - highest)
        total = jnp.sum(raised, axis=1, keepdims=True) + own_raised
        weights = (raised / total).astype(BF16)
        own_weight = (own_raised / total).astype(BF16).astype(F32)
        mixed = dot_nn(weights, vc[r]) + own_weight * widen(v_fresh)
        mixed = mixed.astype(BF16).astype(F32)
        for t in (0, 1):
            out[pl.ds(4 * t + r, pairs, stride=8), :] = mixed[t * pairs : (t + 1) * pairs]


def layer_kernel(
    hidden_ref, gains_ref, lengths, wq_hbm, wk_hbm, wv_hbm, wo_hbm, wg_hbm, wu_hbm, wd_hbm, kc_hbm, vc_hbm,
    out_ref,
    g, wq, wkv, wo, wgu, wd, kc, vc, acc, sbuf, rbuf, near, ysend, yrecv, res,
    qkv, own_part, qkv_s, qkv_r, heads, msgf, msg, rq, rqf, msg2, rq2, attf, att,
    pg, s1, r1, s2, r2, act,
    lsem, gss, grs, ssem, rsem, yss, yrs, wss, wrs, ass, ars, bss, brs,
):
    at = Place()
    width = hidden_ref.shape[1]
    units = wd.shape[0]
    half = width // 2
    loads = [
        pltpu.make_async_copy(src, dst, lsem.at[i])
        for i, (src, dst) in enumerate(
            (
                (wq_hbm, wq),
                (wk_hbm, wkv.at[pl.ds(0, 16)]),
                (wv_hbm, wkv.at[pl.ds(16, 16)]),
                (kc_hbm, kc),
                (vc_hbm, vc),
                (wo_hbm, wo),
                (wg_hbm, wgu.at[0, pl.ds(0, units)]),
                (wu_hbm, wgu.at[1, pl.ds(0, units)]),
                (wd_hbm, wd),
            )
        )
    ]
    for load in loads:
        load.start()
    fill_own(at, g, hidden_ref[...].astype(F32), gains_ref[0:1, :].astype(F32))
    enter(at)
    pairs = ((gss, grs), (ssem, rsem), (yss, yrs), (wss, wrs), (ass, ars), (bss, brs))
    glink, link, ylink, wlink, alink, blink = (Link(a, b, at.partner) for a, b in pairs)
    mates = (at.core_peer, at.y_peer, at.far_peer)
    c_, yl = at.core, at.yl
    tasks = {}

    def add(name, body, cost=0.0):
        tasks[name] = (body, cost)

    def here(c):
        return (at.yh, c)

    def there(c):
        return (at.yh, 1 - c)

    def fresh_zeros():
        wkv[pl.ds(32, 96), :] = jnp.zeros((96, width), BF16)
        for k in (0, 1):
            wgu[k, pl.ds(units, 64), :] = jnp.zeros((64, width), BF16)

    add("zeros", fresh_zeros, 0.6)

    def add_loaded(name, which):
        def body():
            for load in which:
                load.wait()

        add(name, body)

    add_loaded("load_qkv", loads[:3])
    add_loaded("load_cache", loads[3:5])
    add_loaded("load_out", loads[5:6])
    add_loaded("load_mlp", loads[6:])

    def add_gather(turn, c):
        name = f"g{turn}{c}"
        halves = [Gather(at, glink, g, c, f) for f in (0, 1)]

        def slot(f):
            return turn * 4 + c * 2 + f

        def own_rows():
            if turn == 1:
                fill_own(at, g, res[...].astype(F32), gains_ref[1:2, :].astype(F32))
            for f in (0, 1):
                mine = g.at[at.h, :, halves[f].cols]
                like = lambda f=f: g.at[0, :, halves[f].cols]
                ylink.send(slot(f), mine, mine, at.partner, c, like)

        add(f"{name}.own", lambda: only(here(c), own_rows), 0.4 * turn)
        for f in (0, 1):
            def arrive(f=f):
                theirs = g.at[at.partner[1], :, halves[f].cols]
                only(there(c), lambda: ylink.wait(slot(f), theirs, at.partner))

            add(f"{name}.{f}.arrive", arrive)
            halves[f].tasks(add, f"{name}.{f}")

        def end():
            for each in halves:
                each.end()

        def finish():
            for f in (0, 1):
                glink.finish(slots_of(c, f))
            only(here(c), lambda: ylink.finish([slot(0), slot(1)], c))

        add(f"{name}.end", end)
        if turn == 0:
            add(f"{name}.finish", finish)

    def add_scatter(turn, c):
        name = f"s{turn}{c}"
        for f in (0, 1):
            one = Scatter(at, link, acc, sbuf, rbuf, c, f)
            one.tasks(add, f"{name}.{f}")
            slot = 8 + turn * 4 + c * 2 + f
            buf = turn * 2 + f

            def total(one=one, f=f, slot=slot, buf=buf):
                near[c, f] = one.total()

                def pass_over():
                    ysend[buf] = near[c, f].astype(BF16)
                    ylink.send(slot, ysend.at[buf], yrecv.at[buf], at.partner, 1 - c, lambda: ysend.at[buf])

                only(there(c), pass_over)

            def last(f=f, slot=slot, buf=buf):
                def body():
                    cols = pl.ds(f * half, half)
                    ylink.wait(slot, yrecv.at[buf], at.partner)
                    value = near[c, f] + yrecv[buf].astype(F32)
                    if turn == 0:
                        res[:, cols] = (hidden_ref[:, cols].astype(F32) + value).astype(BF16)
                    else:
                        out_ref[:, cols] = (res[:, cols].astype(F32) + value).astype(BF16)

                only(here(c), body)

            add(f"{name}.{f}.total", total, 0.15)
            add(f"{name}.{f}.last", last, 0.1)
            if turn == 0:
                add(f"{name}.{f}.finish", functools.partial(link.finish, slots_of(c, f)))

    def add_attention(c):
        active, passive = (at.yl, c), (at.yl, 1 - c)

        def project():
            rows = g[pl.ds(c * 16, 16), :, pl.ds(0, width)].reshape(256, width)
            extra = g[pl.ds(c * 16, 16), :, pl.ds(width, 128)].reshape(256, 128).astype(F32)
            qkv[:, :, pl.ds(0, 256)] = dot_nn(rows, wq[...]).reshape(2, 128, 256)
            qkv[:, :, pl.ds(256, 128)] = (dot_nt(rows, wkv[...]) + extra).reshape(2, 128, 128)
            buf, like = qkv_s.at[c], lambda: qkv_s.at[c, 0]
            qkv_s[c] = qkv[...].astype(BF16)

            def inside():
                wlink.send(0, buf.at[1 - c_], qkv_r.at[0], at.core_peer, c, like)

            def across():
                wlink.send(1, buf.at[c_], qkv_r.at[1], at.y_peer, 1 - c, like)
                wlink.send(2, buf.at[1 - c_], qkv_r.at[2], at.far_peer, 1 - c, like)

            only(active, inside)
            only(passive, across)
            only(active, lambda: own_part.__setitem__(Ellipsis, qkv[c_]))

        def sum_up():
            total = own_part[...]
            for i, peer in enumerate(mates):
                wlink.wait(i, qkv_r.at[i], peer)
                total = total + qkv_r[i].astype(F32)
            norm = lax.rsqrt(joined_sum(total[:, 256:], lane_ids(128)) / D + norm_eps)
            scaled = (total * norm).astype(BF16)
            row = lax.broadcasted_iota(jnp.int32, (128, 256), 0)
            col = lax.broadcasted_iota(jnp.int32, (128, 256), 1)
            wanted = 16 * (col // 128) + lax.rem(col, 16)
            placed = (row == wanted) & (lax.rem(col, 128) // 16 == lax.rem(at.h, 8))
            fresh = dot_nn(scaled[:, 256:], jnp.where(placed, 1.0, 0.0).astype(BF16))
            heads[0] = scaled[:, :128].astype(F32)
            heads[1] = scaled[:, 128:256].astype(F32)
            heads[2] = fresh[:, :128]
            heads[3] = fresh[:, 128:]
            for t in range(4):
                for r in range(4):
                    msgf[pl.ds(4 * t + r, 32, stride=16), :] = heads[t, pl.ds(r, 32, stride=4), :]
            msg[...] = msgf[...].astype(BF16).reshape(32, 16, 128)
            exchange(at, alink, lambda d: msg.at[d], lambda d: rq.at[d], c, lambda: msg.at[0])
            rq[at.h] = msg[at.h]

        def eight(ref):
            return lambda d: ref.at[pl.ds(pl.multiple_of(d * 8, 8), 8)]

        def attention():
            exchanged(at, alink, lambda d: rq.at[d])
            rqf[...] = rq[...].astype(F32).reshape(512, 128)
            attend(lengths, rqf, kc, vc, msg2)
            exchange(at, blink, eight(msg2), eight(rq2), c, lambda: msg2.at[pl.ds(0, 8)])
            own8 = pl.ds(pl.multiple_of(at.h * 8, 8), 8)
            rq2[own8, :] = msg2[own8, :]

        def hand_out():
            exchanged(at, blink, eight(rq2))
            for t in (0, 1):
                for r in range(4):
                    attf[t, pl.ds(r, 32, stride=4), :] = rq2[pl.ds(4 * t + r, 32, stride=8), :]
                att[at.w, :, pl.ds(t * 128, 128)] = attf[t].astype(BF16)
            for i, peer in enumerate(mates):
                wlink.send(3 + i, att.at[at.w], att.at[at.w], peer, c, lambda: att.at[0])
            alink.finish(None, c)
            blink.finish(None, c)

        def take_in():
            only(active, lambda: wlink.wait(3, att.at[at.core_peer[0]], at.core_peer))

            def across():
                wlink.wait(4, att.at[at.y_peer[0]], at.y_peer)
                wlink.wait(5, att.at[at.far_peer[0]], at.far_peer)

            only(passive, across)

        def out_product(f):
            rows = att[pl.ds(2 * c, 2)].reshape(256, 256)
            for i in (2 * f, 2 * f + 1):
                cols = pl.ds(i * 1024, 1024)
                acc[pl.ds(c * 16, 16), :, cols] = dot_nn(rows, wo[:, cols]).reshape(16, 16, 1024)

        add(f"a{c}.project", project, 0.2)
        add(f"a{c}.sum", lambda: only(active, sum_up), 1.0)
        add(f"a{c}.attend", lambda: only(active, attention), 1.2)
        add(f"a{c}.hand", lambda: only(active, hand_out), 0.3)
        add(f"a{c}.take", take_in)
        for f in (0, 1):
            add(f"a{c}.out{f}", functools.partial(out_product, f))

    def add_mlp(c):
        base = 6 + c * 7
        cuts = ((0, 256), (256, 256), (512, 384))

        def gate_up(k, i):
            start, size = cuts[i]
            rows = g[pl.ds(c * 16, 16), :, pl.ds(0, width)].reshape(256, width)
            value = dot_nt(rows, wgu[k, pl.ds(start, size), :])
            pg[k, c, :, :, pl.ds(start, size)] = value.reshape(4, 64, size)
            if i == 2:
                if k == 0:
                    extra = g[pl.ds(c * 16, 16), :, pl.ds(width, 128)].reshape(4, 64, 128).astype(F32)
                    end = pl.ds(768, 128)
                    pg[0, c, :, :, end] = pg[0, c, :, :, end] + extra
                s1[c, k] = pg[k, c, pl.ds(2 * (1 - c_), 2)].astype(BF16)
                wlink.send(base + k, s1.at[c, k], r1.at[c, k], at.core_peer)

        def over_y(k):
            wlink.wait(base + k, r1.at[c, k], at.core_peer)
            value = pg[k, c, 2 * c_ + 1 - yl] + r1[c, k, 1 - yl].astype(F32)
            s2[c, k] = value.astype(BF16)
            if k == 0:
                lanes = lane_ids(64)
                tile = value[:, 768:]
                s2[c, k, :, pl.ds(768, 128)] = split_sum(joined_sum(tile, lanes), lanes, tile).astype(BF16)
            wlink.send(base + 2 + k, s2.at[c, k], r2.at[c, k], at.y_peer)

        def activate():
            sums = []
            for k in (0, 1):
                wlink.wait(base + 2 + k, r2.at[c, k], at.y_peer)
                sums.append(pg[k, c, 2 * c_ + yl] + r1[c, k, yl].astype(F32) + r2[c, k].astype(F32))
            scale = lax.rsqrt(joined_sum(sums[0][:, 768:], lane_ids(64)) / D + norm_eps)
            gate, up = sums[0][:, :units] * scale, sums[1][:, :units] * scale
            mine = act.at[c, 2 * c_ + yl]
            act[c, 2 * c_ + yl] = (gate / (1.0 + jnp.exp(-gate)) * up).astype(BF16)
            wlink.send(base + 4, mine, mine, at.y_peer)
            wlink.send(base + 5, mine, mine, at.core_peer)

        def pass_on():
            other = act.at[c, 2 * c_ + 1 - yl]
            wlink.wait(base + 4, other, at.y_peer)
            wlink.send(base + 6, other, other, at.core_peer)

        def complete():
            wlink.wait(base + 5, act.at[c, 2 * (1 - c_) + yl], at.core_peer)
            wlink.wait(base + 6, act.at[c, 2 * (1 - c_) + 1 - yl], at.core_peer)

        def down(i):
            rows = act[c].reshape(256, units)
            cols = pl.ds(i * 1024, 1024)
            acc[pl.ds(c * 16, 16), :, cols] = dot_nn(rows, wd[:, cols]).reshape(16, 16, 1024)

        for k in (0, 1):
            for i in range(3):
                add(f"m{c}.gu{k}{i}", functools.partial(gate_up, k, i), 0.25 * (i == 2))
            add(f"m{c}.y{k}", functools.partial(over_y, k), 0.2)
        add(f"m{c}.act", activate, 0.5)
        add(f"m{c}.pass", pass_on)
        add(f"m{c}.complete", complete)
        for i in range(4):
            add(f"m{c}.down{i}", functools.partial(down, i))

    for c in (0, 1):
        add_gather(0, c)
        add_attention(c)
        add_scatter(0, c)
        add_gather(1, c)
        add_mlp(c)
        add_scatter(1, c)

    for name in order_of(tasks):
        enter_task(name, tasks[name][1])
        tasks[name][0]()
    for each in (glink, link, wlink):
        each.finish()
    for c in (0, 1):
        only(here(c), lambda c=c: ylink.finish(None, c))
        only((at.yl, c), lambda c=c: wlink.finish(None, c))


def enter_task(name, cost):
    pass


ORDER = [
    "g00.own", "g01.own", "g00.0.arrive", "g00.0.start", "g00.1.arrive", "g00.1.start", "g01.0.arrive",
    "g01.0.start", "g01.1.arrive", "g00.0.first", "g00.0.second", "g00.1.second", "g00.1.relay0", "zeros",
    "g00.1.first", "g01.1.start", "load_qkv", "g00.0.third", "g00.0.relay1", "g00.0.relay-1", "g00.1.third",
    "g00.0.relay2", "load_out", "g00.1.relay-1", "g00.1.relay1", "g00.0.relay0", "g00.1.relay2",
    "g01.0.first", "g01.1.second", "g01.1.first", "g01.1.relay0", "load_mlp", "g01.0.second", "load_cache",
    "g01.0.relay0", "g01.0.relay1", "g00.end", "g00.finish", "a0.project", "g01.1.third", "g01.1.relay1",
    "g01.0.third", "g01.1.relay-1", "g01.0.relay-1", "g01.1.relay2", "g01.0.relay2", "a0.sum", "g01.end",
    "a1.project", "a0.attend", "a1.sum", "g01.finish", "a0.hand", "a1.attend", "a0.take", "a0.out0",
    "s00.0.far2", "a0.out1", "s00.1.far1", "s00.1.back-1", "s00.0.back1", "s00.1.far2", "s00.0.back0",
    "s00.1.far0", "s00.1.back0", "s00.0.far-1", "s00.1.back2", "s00.1.far-1", "s00.0.back2", "s00.0.far0",
    "a1.hand", "s00.0.far1", "s00.1.back1", "s00.1.on2", "s00.0.back-1", "s00.0.on2", "s00.0.on-1",
    "s00.1.on1", "s00.1.on0", "s00.1.on-1", "s00.0.on1", "s00.0.on0", "s00.0.line_far", "a1.take",
    "s00.1.line_far", "a1.out0", "a1.out1", "s01.0.far2", "s00.0.line_back", "s01.1.far2", "s01.0.far1",
    "s00.0.line_on", "s01.1.back0", "s00.1.line_back", "s00.1.line_on", "s01.0.far-1", "s01.0.far0",
    "s01.1.back1", "s01.1.far1", "s01.0.back1", "s01.1.far-1", "s01.1.on2", "s01.0.back0", "s00.0.total",
    "s01.1.back2", "s01.0.on2", "s01.0.on1", "s01.0.back2", "s00.1.total", "s01.1.back-1", "s01.0.back-1",
    "s01.1.far0", "s01.0.on-1", "s01.1.on-1", "s01.0.on0", "s01.1.on1", "s01.0.line_far", "s01.1.on0",
    "s01.1.line_far", "s01.1.line_back", "s01.0.line_back", "s00.0.last", "s00.1.last", "g10.own",
    "s01.0.line_on", "g10.0.arrive", "g10.0.start", "s01.1.line_on", "g10.1.arrive", "g10.1.start",
    "s01.0.total", "g10.0.first", "s01.0.last", "s01.1.total", "g10.1.first", "s01.1.last", "g10.0.second",
    "g11.own", "g10.1.relay0", "g10.0.third", "s00.0.finish", "g10.1.second", "g10.0.relay-1", "g10.1.third",
    "g10.0.relay2", "g10.0.relay1", "g10.0.relay0", "g10.1.relay1", "g10.1.relay-1", "g10.1.relay2",
    "g11.0.arrive", "g11.1.arrive", "s00.1.finish", "g11.1.start", "g11.0.start", "g10.end", "m0.gu11",
    "m0.gu00", "g11.1.first", "m0.gu10", "g11.0.second", "g11.0.first", "g11.0.relay0", "g11.1.second",
    "m0.gu12", "g11.1.third", "m0.gu01", "m0.y1", "g11.1.relay0", "g11.0.third", "m0.gu02", "g11.0.relay1",
    "g11.1.relay1", "g11.1.relay-1", "m0.y0", "g11.0.relay-1", "g11.0.relay2", "g11.1.relay2", "m0.act",
    "g11.end", "m1.gu00", "m1.gu01", "m1.gu02", "m1.gu10", "m1.y0", "m0.pass", "m1.gu11", "m1.gu12",
    "m0.complete", "m0.down3", "m1.y1", "m0.down2", "s10.1.far2", "m0.down1", "s10.1.far-1", "m0.down0",
    "s10.0.back0", "s10.1.far0", "s10.0.far1", "s10.1.back2", "s10.0.far2", "s10.1.far1", "s10.0.back1",
    "s10.0.far-1", "m1.act", "s10.0.far0", "s10.0.back2", "s10.1.on2", "s10.1.on-1", "s10.1.back1",
    "s10.0.on2", "s10.0.back-1", "s10.1.back0", "s10.1.on1", "s01.0.finish", "s10.0.on1", "m1.pass",
    "s10.1.back-1", "s10.1.on0", "s10.0.on-1", "s10.1.line_far", "m1.complete", "s10.0.on0", "m1.down0",
    "m1.down1", "s11.0.far2", "s10.0.line_far", "s11.0.far-1", "m1.down3", "s01.1.finish", "m1.down2",
    "s11.1.back0", "s11.1.far2", "s10.0.line_back", "s11.1.far1", "s11.0.far1", "s11.0.on2", "s11.0.back0",
    "s11.0.back1", "s11.1.back-1", "s11.0.back2", "s11.1.far-1", "s11.0.far0", "s10.1.line_back",
    "s11.1.far0", "s11.1.on2", "s11.1.back2", "s11.0.on1", "s11.0.back-1", "s10.1.line_on", "s11.1.on-1",
    "s10.0.line_on", "s11.1.back1", "s11.1.on1", "s11.0.on-1", "s11.0.on0", "s11.0.line_far",
    "s11.0.line_back", "s11.1.on0", "s11.1.line_far", "s10.1.total", "s11.0.line_on", "s10.0.total",
    "s11.1.line_back", "s11.1.line_on", "s11.0.total", "s11.0.last", "s11.1.total", "s10.1.last",
    "s10.0.last", "s11.1.last",
]


def order_of(tasks):
    assert sorted(ORDER) == sorted(tasks)
    return ORDER


VM = pl.BlockSpec(memory_space=pltpu.VMEM)
ANY = pl.BlockSpec(memory_space=pl.ANY)
DMA = pltpu.SemaphoreType.DMA


def on_device(
    hidden_in,
    attn_gain,
    mlp_gain,
    w_query,
    w_key,
    w_value,
    w_out,
    w_gate,
    w_up,
    w_down,
    key_cache,
    value_cache,
    lengths,
):
    width = hidden_in.shape[1]
    units = w_gate.shape[1]
    padded = units + 64
    slots = key_cache.shape[1] * KV
    return pl.pallas_call(
        layer_kernel,
        out_shape=jax.ShapeDtypeStruct(hidden_in.shape, BF16),
        in_specs=[VM, VM, pl.BlockSpec(memory_space=pltpu.SMEM)] + [ANY] * 9,
        out_specs=VM,
        scratch_shapes=[
            pltpu.VMEM((32, 16, width + 128), BF16),
            pltpu.VMEM((width, 256), BF16),
            pltpu.VMEM((128, width), BF16),
            pltpu.VMEM((256, width), BF16),
            pltpu.VMEM((2, padded, width), BF16),
            pltpu.VMEM((units, width), BF16),
            pltpu.VMEM((4, slots, HD), BF16),
            pltpu.VMEM((4, slots, HD), BF16),
            pltpu.VMEM((32, 16, width), F32),
            pltpu.VMEM((TREE, 16, width // 2), BF16),
            pltpu.VMEM((TREE, 16, width // 2), BF16),
            pltpu.VMEM((2, 2, 16, width // 2), F32),
            pltpu.VMEM((4, 16, width // 2), BF16),
            pltpu.VMEM((4, 16, width // 2), BF16),
            pltpu.VMEM((16, width), BF16),
            pltpu.VMEM((2, 128, 384), F32),
            pltpu.VMEM((128, 384), F32),
            pltpu.VMEM((2, 2, 128, 384), BF16),
            pltpu.VMEM((3, 128, 384), BF16),
            pltpu.VMEM((4, 128, 128), F32),
            pltpu.VMEM((512, 128), F32),
            pltpu.VMEM((32, 16, 128), BF16),
            pltpu.VMEM((32, 16, 128), BF16),
            pltpu.VMEM((512, 128), F32),
            pltpu.VMEM((256, 128), F32),
            pltpu.VMEM((256, 128), F32),
            pltpu.VMEM((2, 128, 128), F32),
            pltpu.VMEM((4, 128, 256), BF16),
            pltpu.VMEM((2, 2, 4, 64, padded), F32),
            pltpu.VMEM((2, 2, 2, 64, padded), BF16),
            pltpu.VMEM((2, 2, 2, 64, padded), BF16),
            pltpu.VMEM((2, 2, 64, padded), BF16),
            pltpu.VMEM((2, 2, 64, padded), BF16),
            pltpu.VMEM((2, 4, 64, units), BF16),
            DMA((9,)),
            DMA((TREE,)), DMA((TREE,)),
            DMA((TREE,)), DMA((TREE,)),
            DMA((16,)), DMA((16,)),
            DMA((20,)), DMA((20,)),
            DMA((32,)), DMA((32,)),
            DMA((32,)), DMA((32,)),
        ],
        compiler_params=pltpu.CompilerParams(
            collective_id=0, has_side_effects=True, vmem_limit_bytes=63 * 2**20
        ),
    )(
        hidden_in,
        jnp.stack([attn_gain, mlp_gain]),
        lengths,
        w_query,
        w_key.T,
        w_value.T,
        w_out,
        w_gate.T,
        w_up.T,
        w_down,
        key_cache.reshape(4, slots, HD),
        value_cache.reshape(4, slots, HD),
    )


def solution(mesh):
    return jax.shard_map(
        on_device,
        mesh=mesh,
        in_specs=(
            P("hidden", "width"),
            P("width"),
            P("width"),
            P("width", "hidden"),
            P("width", "hidden"),
            P("width", "hidden"),
            P("hidden", "width"),
            P("width", "hidden"),
            P("width", "hidden"),
            P("hidden", "width"),
            P(("width", "hidden"), None, None, None),
            P(("width", "hidden"), None, None, None),
            P(("width", "hidden")),
        ),
        out_specs=P("hidden", "width"),
        check_vma=False,
    )
```

time: 731 us -> 171 us (0.23)
  waiting for transfers between devices: 624 us -> 0 us
  Pallas kernels: 0 us -> 165 us
  matrix products: 36.6 us -> 0 us
  blocking collectives: 31.9 us -> 0 us
  between operations: 13.7 us -> 0.02 us
  other arithmetic: 12.8 us -> 0.65 us
  starting transfers between devices: 9.78 us -> 0 us
    reduce_scatter x3 -> x0, waiting for transfers between devices: 407 us -> none  [the longest x1 198 us: on_device(): lax.psum_scatter(jnp.dot(picked, w_out, preferred_element_type=jnp.float3...]
    pallas_call x0 -> x1, Pallas kernels: none -> 165 us  [on_device(): pl.pallas_call(layer_kernel, out_shape=jax.ShapeDtypeStruct(hidden_in.sha...]
    all_gather x2 -> x0, waiting for transfers between devices: 158 us -> none  [the longest x1 82.5 us: on_device(): block_rows = lax.all_gather(normed, 'hidden', axis=0, tiled=True)]
    psum x1 -> x0, waiting for transfers between devices: 48.7 us -> none  [on_device(): lax.psum(both_parts.astype(jnp.bfloat16), 'width').astype(jnp.float32)]
    dot_general x10 -> x0, matrix products: 36.6 us -> none  [the longest x1 9.24 us: on_device(): jnp.dot(picked, w_down, preferred_element_type=jnp.float32)]
    all_to_all x1 -> x0, blocking collectives: 13.4 us -> none  [on_device(): lax.all_to_all(attended, 'hidden', split_axis=1, concat_axis=0, tiled=True)]
    psum x2 -> x0, blocking collectives: 12.7 us -> none  [normalize(): totals = lax.psum(jnp.sum(widened * widened, axis=1), 'width')]
    all_to_all x1 -> x0, waiting for transfers between devices: 9.76 us -> none  [on_device(): lax.all_to_all(summed, 'hidden', split_axis=0, concat_axis=1, tiled=True)]
  transfers between devices with their start and end apart: 7 -> 0, of which waited for: 7 -> 0; matrix products, arithmetic and copies ran while one was open for 0% -> 0% of each run, Pallas kernels for 0% -> 0%
where the time goes in v3:
time: 171 us; the launch traced here: 169 us
  Pallas kernels  165 us (96%)
  local copies, waits for them, and re-layouts  2.99 us (2%)
    pallas_call x1, Pallas kernels, on_device(): pl.pallas_call(layer_kernel, out_shape=jax.ShapeDtypeStruct(hidden_in.sha...  165 us

profile of v3, /device:TPU:0, one launch (start us, length us, event | category | flops | bytes accessed | tf_op | source)
XLA Modules:
  0.0 168.6 jit_solution(10954143055768675140)
XLA Ops:
  0.0 0.7 stack.9
  0.7 0.7 stack.10
  1.4 0.6 pad_maximum_fusion.gains_ref
  2.1 165.0 %shard_map.127 = bf16[16,4096]{1,0:T(8,128)(2,1)} custom-call(bf16[16,4096]{1,0:T(8,128)(2,1)} %hidden_ref.1, bf16[2,4096]{1,0:T(2,128)(2,1)} %pad_maximum_fusion.gains_ref, s32[4]{0:T(128)} %lengths.1, bf16[4096,256]{1,0:T(8,128)(2,1)} %wq_hbm.1, bf16[16,4096]{1,0:T(8,128)(2,1)} %bitcast.10, bf16[16,4096]{1,0:T(8,128)(2,1)} %bitcast.11, ...), custom_call_target="tpu_custom_call" | custom-call | tf_op jit(solution)/shard_map/pallas_call | solution.py:701
  167.0 1.6 copy.15

commit v4 on v3

v4 whole, which is shorter than its diff:
```python
import functools
import math

import jax
import jax.numpy as jnp
from jax import lax
from jax.experimental import pallas as pl
from jax.experimental.pallas import tpu as pltpu
from jax.sharding import PartitionSpec as P

D = 16384
HEADS = 64
KV = 4
HD = 128
MESH = pl.DeviceIdType.MESH
F32 = jnp.float32
BF16 = jnp.bfloat16

rope_base = 500000.0
norm_eps = 1e-05

OFFS = (0, -1, 1, 2)


class Place:
    def __init__(self):
        self.w = lax.axis_index("width")
        self.h = lax.axis_index("hidden")
        self.x = lax.rem(self.h, 4)
        self.z = lax.rem(self.h // 4, 4)
        self.yh = self.h // 16
        self.core = lax.rem(self.w, 2)
        self.yl = self.w // 2
        self.partner = (self.w, lax.rem(self.h + 16, 32))
        self.core_peer = (self.w + 1 - 2 * self.core, self.h)
        self.y_peer = (lax.rem(self.w + 2, 4), self.h)
        self.far_peer = (lax.rem(self.w + 2, 4) + 1 - 2 * self.core, self.h)

    def block(self, c, f, p, q):
        dx, dz = (p, q) if f == 0 else (q, p)
        return c * 16 + lax.rem(self.z + (dz + 4), 4) * 4 + lax.rem(self.x + (dx + 4), 4)

    def neighbour(self, f, phase, sgn):
        p, q = (sgn, 0) if phase == 0 else (0, sgn)
        return (self.w, self.yh * 16 + self.block(0, f, p, q))

    def along(self, i):
        return (self.w, lax.rem(self.h + i, 32))


def enter(at):
    barrier = pltpu.get_barrier_semaphore()
    peers = [at.core_peer, at.y_peer, at.far_peer] + [at.along(i) for i in range(1, 32)]
    for peer in peers:
        pl.semaphore_signal(barrier, inc=1, device_id=peer, device_id_type=MESH)
    pl.semaphore_wait(barrier, len(peers))


class Link:
    def __init__(self, ssem, rsem, peer):
        self.ssem, self.rsem, self.peer, self.sent = ssem, rsem, peer, {}

    def copy(self, slot, src, dst, peer):
        return pltpu.make_async_remote_copy(
            src_ref=src,
            dst_ref=dst,
            send_sem=self.ssem.at[slot],
            recv_sem=self.rsem.at[slot],
            device_id=peer,
            device_id_type=MESH,
        )

    def send(self, slot, src, dst, peer, key=None, like=None):
        self.copy(slot, src, dst, peer).start()
        self.sent[(slot, key)] = like or (lambda: src)

    def wait(self, slot, dst, peer):
        self.copy(slot, dst, dst, peer).wait_recv()

    def finish(self, slots=None, key=None):
        for which in [w for w in self.sent if w[1] == key and (slots is None or w[0] in slots)]:
            like = self.sent.pop(which)()
            self.copy(which[0], like, like, self.peer).wait_send()


def only(flag, body):
    pl.when(flag[0] == flag[1])(body)


TREE = 60


def slots_of(c, f):
    return range((c * 2 + f) * 15, (c * 2 + f) * 15 + 15)


def slot_of(c, f, phase, j, d):
    base = (c * 2 + f) * 15
    if phase == 0:
        return base + {1: 0, -1: 1, 0: 2}[d]
    return base + 3 + OFFS.index(j) * 3 + {1: 0, -1: 1, 0: 2}[d]


class Gather:
    def __init__(self, at, link, g, c, f):
        half = g.shape[2] // 2 // 128 * 128
        self.cols = pl.ds(0, half) if f == 0 else pl.ds(half, g.shape[2] - half)
        self.at, self.link, self.g, self.c, self.f = at, link, g, c, f
        self.s = 1 if (c ^ f) == 0 else -1

    def ref(self, p, q):
        return self.g.at[self.at.block(self.c, self.f, p, q), :, self.cols]

    def send(self, phase, j, d, p, q, sgn):
        r = self.ref(p, q)
        slot = slot_of(self.c, self.f, phase, j, d)
        self.link.send(slot, r, r, self.at.neighbour(self.f, phase, sgn))

    def wait(self, phase, j, d, p, q, sgn):
        slot = slot_of(self.c, self.f, phase, j, d)
        self.link.wait(slot, self.ref(p, q), self.at.neighbour(self.f, phase, sgn))

    def way(self, j):
        return self.s if j in (0, -self.s) else -self.s

    def spread(self, j):
        self.send(1, j, self.s, j, 0, self.s)
        self.send(1, j, -self.s, j, 0, -self.s)

    def start(self):
        self.send(0, 0, self.s, 0, 0, self.s)
        self.send(0, 0, -self.s, 0, 0, -self.s)
        self.send(0, 0, 0, 0, 0, 2)
        self.spread(0)

    def first(self):
        s = self.s
        self.wait(0, 0, s, -s, 0, s)
        self.spread(-s)

    def second(self):
        s = self.s
        self.wait(0, 0, -s, s, 0, -s)
        self.spread(s)

    def third(self):
        self.wait(0, 0, 0, 2, 0, 2)
        self.spread(2)

    def relay(self, j):
        s = self.way(j)
        self.wait(1, j, s, j, -s, s)
        self.send(1, j, 0, j, -s, s)

    def end(self):
        for j in OFFS:
            s = self.way(j)
            self.wait(1, j, -s, j, s, -s)
        for j in OFFS:
            self.wait(1, j, 0, j, 2, self.way(j))

    def tasks(self, add, name):
        add(f"{name}.start", self.start)
        add(f"{name}.first", self.first)
        add(f"{name}.second", self.second)
        add(f"{name}.third", self.third)
        for j in (0, -self.s, self.s, 2):
            add(f"{name}.relay{j}", functools.partial(self.relay, j))


class Scatter:
    def __init__(self, at, link, acc, sbuf, rbuf, c, f):
        half = acc.shape[2] // 2
        self.cols = pl.ds(f * half, half)
        self.at, self.link, self.acc, self.sbuf, self.rbuf, self.c, self.f = at, link, acc, sbuf, rbuf, c, f
        self.s = 1 if (c ^ f) == 0 else -1

    def own(self, p, q):
        return self.acc[self.at.block(self.c, self.f, p, q), :, self.cols]

    def send(self, phase, j, d, sgn, value):
        slot = slot_of(self.c, self.f, phase, j, d)
        self.sbuf[slot] = value.astype(BF16)
        self.link.send(slot, self.sbuf.at[slot], self.rbuf.at[slot], self.at.neighbour(self.f, phase, sgn))

    def take(self, phase, j, d, sgn):
        slot = slot_of(self.c, self.f, phase, j, d)
        self.link.wait(slot, self.rbuf.at[slot], self.at.neighbour(self.f, phase, sgn))
        return self.rbuf[slot].astype(F32)

    def way(self, j):
        return self.s if j in (0, -self.s) else -self.s

    def column(self, j):
        s = self.way(j)
        return self.own(j, 0) + self.take(1, j, s, s) + self.take(1, j, -s, -s)

    def far(self, j):
        self.send(1, j, 0, self.way(j), self.own(j, 2))

    def back(self, j):
        s = self.way(j)
        self.send(1, j, -s, -s, self.own(j, -s))

    def on(self, j):
        s = self.way(j)
        self.send(1, j, s, s, self.own(j, s) + self.take(1, j, 0, s))

    def line_far(self):
        self.send(0, 0, 0, 2, self.column(2))

    def line_back(self):
        self.send(0, 0, -self.s, -self.s, self.column(-self.s))

    def line_on(self):
        self.send(0, 0, self.s, self.s, self.column(self.s))

    def total(self):
        value = self.column(0)
        for d, sgn in ((self.s, self.s), (-self.s, -self.s), (0, 2)):
            value = value + self.take(0, 0, d, sgn)
        return value

    def tasks(self, add, name):
        order = (2, -self.s, self.s, 0)
        for j in order:
            add(f"{name}.far{j}", functools.partial(self.far, j), 0.06)
        for j in order:
            add(f"{name}.back{j}", functools.partial(self.back, j), 0.06)
        for j in order:
            add(f"{name}.on{j}", functools.partial(self.on, j), 0.08)
        add(f"{name}.line_far", self.line_far, 0.1)
        add(f"{name}.line_back", self.line_back, 0.1)
        add(f"{name}.line_on", self.line_on, 0.1)


def dot_nn(a, b):
    return jnp.dot(a, b, preferred_element_type=F32)


def dot_nt(a, b):
    return lax.dot_general(a, b, (((1,), (1,)), ((), ())), preferred_element_type=F32)


SS = 96


def split_sum(total, lanes, rest):
    high = total.astype(BF16).astype(F32)
    return jnp.where(lanes == SS, high, jnp.where(lanes == SS + 1, total - high, rest))


def joined_sum(tile, lanes):
    return jnp.sum(jnp.where((lanes == SS) | (lanes == SS + 1), tile, 0.0), axis=1, keepdims=True)


def lane_ids(rows):
    return lax.broadcasted_iota(jnp.int32, (rows, 128), 1)


def fill_own(g, block, values, gain, f):
    width = values.shape[1]
    tiles = width // 256
    for i in range(f * tiles, (f + 1) * tiles):
        cols = pl.ds(i * 128, 128)
        g[block, :, cols] = (values[:, i * 128 : (i + 1) * 128] * gain[i : i + 1]).astype(BF16)
    if f == 1:
        part = jnp.sum(values * values, axis=1, keepdims=True)
        lanes = lane_ids(values.shape[0])
        tail = split_sum(part, lanes, jnp.zeros(lanes.shape, F32))
        g[block, :, pl.ds(width, 128)] = tail.astype(BF16)


def exchange(at, link, src, dst, key, like):
    for i in range(1, 32):
        peer = at.along(i)
        link.send(0, src(peer[1]), dst(at.h), peer, key, like)


def exchanged(at, link, blocks):
    link.wait(0, blocks, at.partner)


def turn(values, cosine, sine):
    return values * cosine + pltpu.roll(values, HD // 2, 1) * sine


def attend(lengths, rqf, kc, vc, out):
    pairs = HEADS // 2
    lane = lax.broadcasted_iota(jnp.int32, (1, HD), 1)
    entry = lax.rem(lane, HD // 2).astype(F32)
    frequency = jnp.exp(entry * (-2.0 * math.log(rope_base) / HD))
    count = kc.shape[1]
    place = lax.broadcasted_iota(jnp.int32, (HEADS, count), 1)
    head_group = lax.rem(lax.broadcasted_iota(jnp.int32, (HEADS, count), 0), pairs) // (pairs // KV)
    same_group = lax.rem(place, KV) == head_group
    slot = place // KV
    factor = HD ** (-0.5)

    def widen(fresh):
        each = jnp.broadcast_to(fresh[:, None, :], (KV, pairs // KV, HD)).reshape(pairs, HD)
        return jnp.concatenate([each, each], axis=0)

    for r in range(4):
        def piece(t):
            return rqf[pl.ds(4 * t + r, pairs, stride=16), :]

        position = lengths[r]
        angle = frequency * position.astype(F32)
        cosine = jnp.cos(angle)
        sine = jnp.where(lane < HD // 2, -1.0, 1.0) * jnp.sin(angle)
        q = turn(jnp.concatenate([piece(0), piece(1)], axis=0), cosine, sine).astype(BF16)
        k_fresh = jnp.sum(piece(2).reshape(KV, pairs // KV, HD), axis=1)
        v_fresh = jnp.sum(piece(3).reshape(KV, pairs // KV, HD), axis=1)
        k_turned = turn(k_fresh, cosine, sine).astype(BF16).astype(F32)
        own = jnp.sum(q.astype(F32) * widen(k_turned), axis=1, keepdims=True) * factor
        visible = same_group & (slot < position)
        scores = jnp.where(visible, dot_nt(q, kc[r]) * factor, -jnp.inf)
        highest = jnp.maximum(jnp.max(scores, axis=1, keepdims=True), own)
        raised = jnp.exp(scores - highest)
        own_raised = jnp.exp(own - highest)
        total = jnp.sum(raised, axis=1, keepdims=True) + own_raised
        weights = (raised / total).astype(BF16)
        own_weight = (own_raised / total).astype(BF16).astype(F32)
        mixed = dot_nn(weights, vc[r]) + own_weight * widen(v_fresh)
        mixed = mixed.astype(BF16).astype(F32)
        for t in (0, 1):
            out[pl.ds(4 * t + r, pairs, stride=8), :] = mixed[t * pairs : (t + 1) * pairs]


def layer_kernel(
    hidden_ref, gain0, gain1, lengths, wq_hbm, wk_hbm, wv_hbm, wo_hbm, wg_hbm, wu_hbm, wd_hbm, kc_hbm, vc_hbm,
    out_ref,
    g, wq, wkv, wo, wgu, wd, kc, vc, acc, sbuf, rbuf, near, ysend, yrecv, res, hid,
    qkv, qkv_s, qkv_r, qkv_y, heads, msgf, msg, rq, rqf, msg2, rq2, attf, att,
    pg, s1, r1, s2, r2, act, scale,
    lsem, gss, grs, ssem, rsem, yss, yrs, wss, wrs, ass, ars, bss, brs,
):
    at = Place()
    width = hidden_ref.shape[1]
    units = wd_hbm.shape[0]
    half = width // 2
    loads = [
        pltpu.make_async_copy(src, dst, lsem.at[i])
        for i, (src, dst) in enumerate(
            (
                (wq_hbm, wq),
                (wk_hbm, wkv.at[pl.ds(0, 16)]),
                (wv_hbm, wkv.at[pl.ds(16, 16)]),
                (kc_hbm, kc),
                (vc_hbm, vc),
                (wo_hbm, wo),
                (wg_hbm, wgu.at[0, pl.ds(0, units)]),
                (wu_hbm, wgu.at[1, pl.ds(0, units)]),
                (wd_hbm, wd.at[pl.ds(0, units)]),
            )
        )
    ]
    for load in loads:
        load.start()
    hid[at.yh] = hidden_ref[...]
    for f in (0, 1):
        fill_own(g, at.h, hidden_ref[...].astype(F32), gain0[...].astype(F32), f)
    enter(at)
    pairs = ((gss, grs), (ssem, rsem), (yss, yrs), (wss, wrs), (ass, ars), (bss, brs))
    glink, link, ylink, wlink, alink, blink = (Link(a, b, at.partner) for a, b in pairs)
    c_, yl = at.core, at.yl
    tasks = {}

    def add(name, body, cost=0.0):
        tasks[name] = (body, cost)

    def here(c):
        return (at.yh, c)

    def there(c):
        return (at.yh, 1 - c)

    def fresh_zeros():
        wkv[pl.ds(32, 96), :] = jnp.zeros((96, width), BF16)
        for k in (0, 1):
            wgu[k, pl.ds(units, 64), :] = jnp.zeros((64, width), BF16)
        wd[pl.ds(units, 64), :] = jnp.zeros((64, width), BF16)

    add("zeros", fresh_zeros, 0.6)

    def swap_hidden():
        mine = hid.at[at.yh]
        ylink.send(8, mine, mine, at.partner)

    def hidden_there():
        theirs = hid.at[1 - at.yh]
        ylink.wait(8, theirs, at.partner)

    add("zh_send", swap_hidden)
    add("zh_wait", hidden_there)

    def add_loaded(name, which):
        def body():
            for load in which:
                load.wait()

        add(name, body)

    add_loaded("load_qkv", loads[:3])
    add_loaded("load_cache", loads[3:5])
    add_loaded("load_out", loads[5:6])
    add_loaded("load_mlp", loads[6:])

    def add_gather(turn, c):
        name = f"g{turn}{c}"
        halves = [Gather(at, glink, g, c, f) for f in (0, 1)]

        def slot(f):
            return c * 2 + f

        def own_rows():
            for f in (0, 1):
                mine = g.at[at.h, :, halves[f].cols]
                like = lambda f=f: g.at[0, :, halves[f].cols]
                ylink.send(slot(f), mine, mine, at.partner, c, like)

        def new_rows(f):
            fill_own(g, at.block(c, 0, 0, 0), res[c].astype(F32), gain1[...].astype(F32), f)

        if turn == 0:
            add(f"{name}.own", lambda: only(here(c), own_rows))
        else:
            for f in (0, 1):
                add(f"{name}.{f}.own", functools.partial(new_rows, f), 0.2)
        for f in (0, 1):
            def arrive(f=f):
                theirs = g.at[at.partner[1], :, halves[f].cols]
                only(there(c), lambda: ylink.wait(slot(f), theirs, at.partner))

            if turn == 0:
                add(f"{name}.{f}.arrive", arrive)
            halves[f].tasks(add, f"{name}.{f}")

        def finish():
            for f in (0, 1):
                glink.finish(slots_of(c, f))
            only(here(c), lambda: ylink.finish([slot(0), slot(1)], c))

        for f in (0, 1):
            add(f"{name}.{f}.end", halves[f].end)
        if turn == 0:
            add(f"{name}.finish", finish)

    def add_scatter(turn, c):
        name = f"s{turn}{c}"
        for f in (0, 1):
            one = Scatter(at, link, acc, sbuf, rbuf, c, f)
            one.tasks(add, f"{name}.{f}")
            slot = 4 + c * 2 + f if turn == 0 else 9 + f
            buf = c * 2 + f if turn == 0 else 4 + f
            cols = pl.ds(f * half, half)

            def total(one=one, f=f, slot=slot, buf=buf):
                near[c, f] = one.total()

                def pass_over():
                    ysend[buf] = near[c, f].astype(BF16)
                    ylink.send(slot, ysend.at[buf], yrecv.at[buf], at.partner, 1 - c, lambda: ysend.at[buf])

                if turn == 0:
                    ysend[buf] = near[c, f].astype(BF16)
                    ylink.send(slot, ysend.at[buf], yrecv.at[buf], at.partner)
                else:
                    only(there(c), pass_over)

            def last(f=f, slot=slot, buf=buf, cols=cols):
                def body():
                    ylink.wait(slot, yrecv.at[buf], at.partner)
                    value = near[c, f] + yrecv[buf].astype(F32)
                    out_ref[:, cols] = (res[c, :, cols].astype(F32) + value).astype(BF16)

                if turn == 0:
                    ylink.wait(slot, yrecv.at[buf], at.partner)
                    value = ysend[buf].astype(F32) + yrecv[buf].astype(F32)
                    res[c, :, cols] = (hid[c, :, cols].astype(F32) + value).astype(BF16)
                else:
                    only(here(c), body)

            add(f"{name}.{f}.total", total, 0.15)
            add(f"{name}.{f}.last", last, 0.1)
            if turn == 0:
                add(f"{name}.{f}.finish", functools.partial(link.finish, slots_of(c, f)))

    def add_attention(c):
        active, passive = (at.yl, c), (at.yl, 1 - c)

        def project(f):
            cols = pl.ds(f * half, half)
            rows = g[pl.ds(c * 16, 16), :, cols].reshape(256, half)
            query = dot_nn(rows, wq[cols, :]).reshape(2, 128, 256)
            fresh = dot_nt(rows, wkv[:, cols]).reshape(2, 128, 128)
            if f == 0:
                qkv[c, :, :, pl.ds(0, 256)] = query
                qkv[c, :, :, pl.ds(256, 128)] = fresh
                return
            extra = g[pl.ds(c * 16, 16), :, pl.ds(width, 128)].reshape(2, 128, 128).astype(F32)
            qkv[c, :, :, pl.ds(0, 256)] += query
            qkv[c, :, :, pl.ds(256, 128)] += fresh + extra
            qkv_s[c] = qkv[c, 1 - c_].astype(BF16)
            wlink.send(2 * c, qkv_s.at[c], qkv_r.at[2 * c], at.core_peer)

        def over_y():
            def across():
                wlink.wait(2 * c, qkv_r.at[2 * c], at.core_peer)
                total = qkv[c, c_] + qkv_r[2 * c].astype(F32)
                lanes = lane_ids(128)
                tile = total[:, 256:]
                qkv_y[:, pl.ds(0, 256)] = total[:, :256].astype(BF16)
                qkv_y[:, pl.ds(256, 128)] = split_sum(joined_sum(tile, lanes), lanes, tile).astype(BF16)
                wlink.send(1, qkv_y, qkv_r.at[1], at.y_peer, 1 - c, lambda: qkv_y)

            only(passive, across)

        def sum_up():
            total = qkv[c, c_]
            for i, peer in ((2 * c, at.core_peer), (1, at.y_peer)):
                wlink.wait(i, qkv_r.at[i], peer)
                total = total + qkv_r[i].astype(F32)
            norm = lax.rsqrt(joined_sum(total[:, 256:], lane_ids(128)) / D + norm_eps)
            scaled = (total * norm).astype(BF16)
            row = lax.broadcasted_iota(jnp.int32, (128, 256), 0)
            col = lax.broadcasted_iota(jnp.int32, (128, 256), 1)
            wanted = 16 * (col // 128) + lax.rem(col, 16)
            placed = (row == wanted) & (lax.rem(col, 128) // 16 == lax.rem(at.h, 8))
            fresh = dot_nn(scaled[:, 256:], jnp.where(placed, 1.0, 0.0).astype(BF16))
            heads[0] = scaled[:, :128].astype(F32)
            heads[1] = scaled[:, 128:256].astype(F32)
            heads[2] = fresh[:, :128]
            heads[3] = fresh[:, 128:]
            for t in range(4):
                for r in range(4):
                    msgf[pl.ds(4 * t + r, 32, stride=16), :] = heads[t, pl.ds(r, 32, stride=4), :]
            msg[...] = msgf[...].astype(BF16).reshape(32, 16, 128)
            exchange(at, alink, lambda d: msg.at[d], lambda d: rq.at[d], c, lambda: msg.at[pl.ds(0, 31)])

        def eight(ref):
            return lambda d: ref.at[pl.ds(pl.multiple_of(d * 8, 8), 8)]

        def attention():
            exchanged(at, alink, rq.at[pl.ds(0, 31)])
            rq[at.h] = msg[at.h]
            rqf[...] = rq[...].astype(F32).reshape(512, 128)
            attend(lengths, rqf, kc, vc, msg2)
            exchange(at, blink, eight(msg2), eight(rq2), c, lambda: msg2.at[pl.ds(0, 248)])

        def hand_out():
            exchanged(at, blink, rq2.at[pl.ds(0, 248)])
            own8 = pl.ds(pl.multiple_of(at.h * 8, 8), 8)
            rq2[own8, :] = msg2[own8, :]
            for t in (0, 1):
                for r in range(4):
                    attf[t, pl.ds(r, 32, stride=4), :] = rq2[pl.ds(4 * t + r, 32, stride=8), :]
                att[at.w, :, pl.ds(t * 128, 128)] = attf[t].astype(BF16)
            for i, peer in enumerate((at.core_peer, at.y_peer)):
                wlink.send(3 + i, att.at[at.w], att.at[at.w], peer, c, lambda: att.at[0])
            alink.finish(None, c)
            blink.finish(None, c)

        def take_in():
            only(active, lambda: wlink.wait(3, att.at[at.core_peer[0]], at.core_peer))

            def across():
                part = att.at[at.y_peer[0]]
                wlink.wait(4, part, at.y_peer)
                wlink.send(5, part, part, at.core_peer, 1 - c, lambda: att.at[0])

            only(passive, across)

        def take_other():
            only(passive, lambda: wlink.wait(5, att.at[at.far_peer[0]], at.core_peer))

        def out_product(f):
            rows = att[pl.ds(2 * c, 2)].reshape(256, 256)
            for i in (2 * f, 2 * f + 1):
                cols = pl.ds(i * 1024, 1024)
                acc[pl.ds(c * 16, 16), :, cols] = dot_nn(rows, wo[:, cols]).reshape(16, 16, 1024)

        for f in (0, 1):
            add(f"a{c}.project{f}", functools.partial(project, f), 0.1 * f)
        add(f"a{c}.over", over_y, 0.25)
        add(f"a{c}.sum", lambda: only(active, sum_up), 1.0)
        add(f"a{c}.attend", lambda: only(active, attention), 1.2)
        add(f"a{c}.hand", lambda: only(active, hand_out), 0.3)
        add(f"a{c}.take", take_in)
        add(f"a{c}.other", take_other)
        for f in (0, 1):
            add(f"a{c}.out{f}", functools.partial(out_product, f))

    def add_mlp(c):
        cuts = ((0, 256), (256, 256), (512, 384))

        def slot(i, which):
            return 6 + (c * 3 + i) * 7 + which

        def gate_up(k, i, f):
            cols, depth = pl.ds(*cuts[i]), pl.ds(f * half, half)
            rows = g[pl.ds(c * 16, 16), :, depth].reshape(256, half)
            value = dot_nt(rows, wgu[k, cols, depth]).reshape(4, 64, cuts[i][1])
            if f == 0:
                pg[k, c, :, :, cols] = value
                return
            pg[k, c, :, :, cols] += value
            if i == 2 and k == 0:
                extra = g[pl.ds(c * 16, 16), :, pl.ds(width, 128)].reshape(4, 64, 128).astype(F32)
                pg[0, c, :, :, pl.ds(768, 128)] += extra
            s1[c, k, :, :, cols] = pg[k, c, pl.ds(2 * (1 - c_), 2), :, cols].astype(BF16)
            wlink.send(slot(i, k), s1.at[c, k, :, :, cols], r1.at[c, k, :, :, cols], at.core_peer)

        def over_y(k, i):
            cols = pl.ds(*cuts[i])
            wlink.wait(slot(i, k), r1.at[c, k, :, :, cols], at.core_peer)
            value = pg[k, c, 2 * c_ + 1 - yl, :, cols] + r1[c, k, 1 - yl, :, cols].astype(F32)
            s2[c, k, :, cols] = value.astype(BF16)
            if i == 2 and k == 0:
                lanes = lane_ids(64)
                tile = value[:, 256:]
                s2[c, k, :, pl.ds(768, 128)] = split_sum(joined_sum(tile, lanes), lanes, tile).astype(BF16)
            wlink.send(slot(i, 2 + k), s2.at[c, k, :, cols], r2.at[c, k, :, cols], at.y_peer)

        def activate(i):
            cols = pl.ds(*cuts[i])
            sums = []
            for k in (0, 1):
                wlink.wait(slot(i, 2 + k), r2.at[c, k, :, cols], at.y_peer)
                total = pg[k, c, 2 * c_ + yl, :, cols] + r1[c, k, yl, :, cols].astype(F32)
                sums.append(total + r2[c, k, :, cols].astype(F32))
            if i == 2:
                norm = lax.rsqrt(joined_sum(sums[0][:, 256:], lane_ids(64)) / D + norm_eps)
                scale[c] = jnp.broadcast_to(norm, (64, 128))
            norm = scale[c, :, 0:1]
            gate, up = sums[0] * norm, sums[1] * norm
            mine = act.at[c, 2 * c_ + yl, :, cols]
            act[c, 2 * c_ + yl, :, cols] = (gate / (1.0 + jnp.exp(-gate)) * up).astype(BF16)
            wlink.send(slot(i, 4), mine, mine, at.y_peer)
            wlink.send(slot(i, 5), mine, mine, at.core_peer)

        def pass_on(i):
            other = act.at[c, 2 * c_ + 1 - yl, :, pl.ds(*cuts[i])]
            wlink.wait(slot(i, 4), other, at.y_peer)
            wlink.send(slot(i, 6), other, other, at.core_peer)

        def complete():
            for i in range(3):
                cols = pl.ds(*cuts[i])
                wlink.wait(slot(i, 5), act.at[c, 2 * (1 - c_) + yl, :, cols], at.core_peer)
                wlink.wait(slot(i, 6), act.at[c, 2 * (1 - c_) + 1 - yl, :, cols], at.core_peer)

        def down(i):
            rows = act[c].reshape(256, act.shape[3])
            cols = pl.ds(i * 1024, 1024)
            acc[pl.ds(c * 16, 16), :, cols] = dot_nn(rows, wd[:, cols]).reshape(16, 16, 1024)

        for i in (2, 0, 1):
            for k in (0, 1):
                for f in (0, 1):
                    add(f"m{c}.gu{k}{i}{f}", functools.partial(gate_up, k, i, f), 0.03 + 0.06 * f)
                add(f"m{c}.y{k}{i}", functools.partial(over_y, k, i), 0.07)
            add(f"m{c}.act{i}", functools.partial(activate, i), 0.2)
            add(f"m{c}.pass{i}", functools.partial(pass_on, i))
        add(f"m{c}.complete", complete)
        for i in range(4):
            add(f"m{c}.down{i}", functools.partial(down, i))

    for c in (0, 1):
        add_gather(0, c)
        add_attention(c)
        add_scatter(0, c)
        add_gather(1, c)
        add_mlp(c)
        add_scatter(1, c)

    for name in order_of(tasks):
        enter_task(name, tasks[name][1])
        tasks[name][0]()
    for each in (glink, link, ylink, wlink):
        each.finish()
    for c in (0, 1):
        only(here(c), lambda c=c: ylink.finish(None, c))
        only((at.yl, c), lambda c=c: wlink.finish(None, c))


def enter_task(name, cost):
    pass


ORDER = [
    "load_qkv", "g01.own", "load_cache", "g00.own", "g00.0.arrive", "g00.0.start", "g00.1.arrive",
    "g00.1.start", "g01.0.arrive", "g01.0.start", "g00.0.first", "g00.1.second", "g00.0.second",
    "g00.1.first", "g00.0.third", "g00.0.relay0", "g00.0.relay-1", "g00.1.third", "g01.1.arrive",
    "g01.1.start", "g00.1.relay-1", "g00.0.relay1", "g00.1.relay0", "g00.0.relay2", "g00.1.relay1",
    "g01.0.third", "g00.1.relay2", "zeros", "g01.1.relay0", "g01.1.first", "load_mlp", "g01.0.second",
    "g01.1.second", "g01.0.first", "g00.0.end", "a0.project0", "g00.1.end", "a0.project1", "g01.1.third",
    "a0.over", "g01.0.relay0", "g01.0.relay2", "zh_send", "g01.0.relay-1", "g01.1.relay1", "g01.0.relay1",
    "load_out", "g01.1.relay-1", "g01.1.relay2", "a0.sum", "g00.finish", "g01.0.end", "a1.project0",
    "g01.1.end", "a1.project1", "a1.over", "a0.attend", "a1.sum", "a0.hand", "a1.attend", "a0.take",
    "a0.other", "a0.out0", "s00.0.far2", "a0.out1", "s00.1.far0", "s00.1.far2", "s00.0.far1", "s00.0.back-1",
    "g01.finish", "s00.1.back0", "s00.0.far-1", "s00.1.far1", "s00.0.far0", "a1.hand", "s00.1.far-1",
    "s00.0.back1", "s00.1.back2", "s00.0.on2", "s00.1.on0", "s00.1.on2", "s00.0.back2", "s00.1.back1",
    "s00.0.on1", "s00.1.on1", "s00.0.on-1", "s00.1.back-1", "s00.0.back0", "s00.0.on0", "s00.1.on-1",
    "a1.take", "a1.other", "a1.out0", "s01.0.far1", "a1.out1", "s00.0.line_far", "s01.1.far2", "s01.0.far2",
    "s01.0.far-1", "s00.0.line_on", "s00.1.line_far", "s01.1.far-1", "s00.1.line_back", "s00.0.line_back",
    "s00.1.line_on", "s01.1.far1", "s01.1.far0", "s01.1.back2", "s01.0.back0", "s01.0.far0", "s01.1.back-1",
    "s01.1.on2", "s01.0.on2", "s01.0.back1", "s01.0.back2", "s01.0.on1", "s00.0.total", "s01.0.on-1",
    "s01.1.on1", "s01.1.back0", "s01.1.on-1", "s00.1.total", "s01.1.back1", "s01.0.back-1", "s01.0.on0",
    "s01.1.on0", "s01.0.line_far", "s01.1.line_far", "zh_wait", "s01.0.line_back", "s01.1.line_back",
    "s01.0.line_on", "s01.1.line_on", "s00.0.last", "g10.0.own", "g10.0.start", "s00.1.last", "g10.1.own",
    "g10.1.start", "s01.0.total", "g10.0.second", "g10.0.first", "s01.1.total", "g10.1.first", "g10.0.third",
    "g10.1.second", "g10.0.relay0", "g10.1.third", "g10.0.relay-1", "s01.0.last", "g11.0.own", "g11.0.start",
    "g10.0.relay1", "s01.1.last", "g10.1.relay0", "g11.1.own", "g10.1.relay1", "g10.0.relay2", "g11.1.start",
    "g10.1.relay-1", "g10.1.relay2", "g11.0.second", "g10.0.end", "g11.0.third", "g11.1.relay0",
    "g11.0.first", "m0.gu120", "m0.gu000", "g11.1.first", "g11.1.second", "m0.gu020", "s00.1.finish",
    "m0.gu100", "g10.1.end", "m0.gu121", "g11.1.third", "s00.0.finish", "m0.gu021", "g11.0.relay-1",
    "g11.0.relay0", "m0.y12", "m0.gu101", "m0.gu001", "g11.0.relay2", "m0.y02", "g11.0.relay1", "m0.gu110",
    "m0.gu010", "m0.gu011", "s01.0.finish", "m0.y10", "m0.gu111", "g11.1.relay1", "m0.y00", "m0.y01",
    "g11.1.relay-1", "m0.y11", "g11.1.relay2", "m0.act2", "g11.0.end", "m1.gu110", "m1.gu010", "m1.gu000",
    "m1.gu020", "m0.act0", "m1.gu120", "m0.act1", "g11.1.end", "m1.gu111", "m1.gu021", "m1.gu121", "m1.y11",
    "m1.gu011", "m1.y02", "m1.gu001", "m0.pass1", "m0.pass2", "m0.pass0", "s01.1.finish", "m1.y12",
    "m1.gu100", "m1.gu101", "m1.y01", "m1.y00", "m0.complete", "m0.down1", "m1.y10", "m0.down0", "s10.0.far1",
    "s10.0.far0", "m0.down2", "m0.down3", "s10.1.far2", "m1.act2", "s10.0.far-1", "s10.1.far0", "s10.0.far2",
    "s10.1.far-1", "m1.act1", "s10.1.far1", "s10.0.back2", "s10.0.back-1", "s10.0.back1", "m1.act0",
    "s10.1.back-1", "s10.1.back1", "s10.1.back2", "s10.0.on1", "s10.1.back0", "m1.pass1", "s10.0.on-1",
    "s10.1.on2", "s10.0.back0", "m1.pass0", "m1.pass2", "s10.1.on0", "s10.0.on0", "s10.1.on1", "s10.0.on2",
    "s10.1.on-1", "m1.complete", "m1.down0", "m1.down1", "s11.0.far2", "s11.0.far1", "m1.down3", "m1.down2",
    "s11.1.far2", "s11.1.far-1", "s11.0.far-1", "s11.0.back2", "s11.0.back0", "s11.1.far0", "s11.0.far0",
    "s10.1.line_far", "s11.1.back2", "s11.1.far1", "s11.1.back-1", "s10.1.line_on", "s10.1.line_back",
    "s11.0.back-1", "s11.0.back1", "s11.0.on1", "s10.0.line_on", "s11.0.on2", "s11.1.on2", "s11.1.on-1",
    "s11.1.on1", "s11.1.back1", "s10.0.line_far", "s10.0.line_back", "s11.1.on0", "s11.1.back0", "s11.0.on0",
    "s11.0.on-1", "s11.1.line_far", "s11.0.line_far", "s10.1.total", "s11.1.line_on", "s11.1.line_back",
    "s11.0.line_on", "s11.0.line_back", "s10.0.total", "s11.1.total", "s11.0.total", "s10.1.last",
    "s11.1.last", "s10.0.last", "s11.0.last",
]


def order_of(tasks):
    assert sorted(ORDER) == sorted(tasks)
    return ORDER


VM = pl.BlockSpec(memory_space=pltpu.VMEM)
ANY = pl.BlockSpec(memory_space=pl.ANY)
DMA = pltpu.SemaphoreType.DMA


def on_device(
    hidden_in,
    attn_gain,
    mlp_gain,
    w_query,
    w_key,
    w_value,
    w_out,
    w_gate,
    w_up,
    w_down,
    key_cache,
    value_cache,
    lengths,
):
    width = hidden_in.shape[1]
    units = w_gate.shape[1]
    padded = units + 64
    slots = key_cache.shape[1] * KV
    return pl.pallas_call(
        layer_kernel,
        out_shape=jax.ShapeDtypeStruct(hidden_in.shape, BF16),
        in_specs=[VM, VM, VM, pl.BlockSpec(memory_space=pltpu.SMEM)] + [ANY] * 9,
        out_specs=VM,
        scratch_shapes=[
            pltpu.VMEM((32, 16, width + 128), BF16),
            pltpu.VMEM((width, 256), BF16),
            pltpu.VMEM((128, width), BF16),
            pltpu.VMEM((256, width), BF16),
            pltpu.VMEM((2, padded, width), BF16),
            pltpu.VMEM((padded, width), BF16),
            pltpu.VMEM((4, slots, HD), BF16),
            pltpu.VMEM((4, slots, HD), BF16),
            pltpu.VMEM((32, 16, width), F32),
            pltpu.VMEM((TREE, 16, width // 2), BF16),
            pltpu.VMEM((TREE, 16, width // 2), BF16),
            pltpu.VMEM((2, 2, 16, width // 2), F32),
            pltpu.VMEM((6, 16, width // 2), BF16),
            pltpu.VMEM((6, 16, width // 2), BF16),
            pltpu.VMEM((2, 16, width), BF16),
            pltpu.VMEM((2, 16, width), BF16),
            pltpu.VMEM((2, 2, 128, 384), F32),
            pltpu.VMEM((2, 128, 384), BF16),
            pltpu.VMEM((3, 128, 384), BF16),
            pltpu.VMEM((128, 384), BF16),
            pltpu.VMEM((4, 128, 128), F32),
            pltpu.VMEM((512, 128), F32),
            pltpu.VMEM((32, 16, 128), BF16),
            pltpu.VMEM((32, 16, 128), BF16),
            pltpu.VMEM((512, 128), F32),
            pltpu.VMEM((256, 128), F32),
            pltpu.VMEM((256, 128), F32),
            pltpu.VMEM((2, 128, 128), F32),
            pltpu.VMEM((4, 128, 256), BF16),
            pltpu.VMEM((2, 2, 4, 64, padded), F32),
            pltpu.VMEM((2, 2, 2, 64, padded), BF16),
            pltpu.VMEM((2, 2, 2, 64, padded), BF16),
            pltpu.VMEM((2, 2, 64, padded), BF16),
            pltpu.VMEM((2, 2, 64, padded), BF16),
            pltpu.VMEM((2, 4, 64, padded), BF16),
            pltpu.VMEM((2, 64, 128), F32),
            DMA((9,)),
            DMA((TREE,)), DMA((TREE,)),
            DMA((TREE,)), DMA((TREE,)),
            DMA((16,)), DMA((16,)),
            DMA((48,)), DMA((48,)),
            DMA((1,)), DMA((1,)),
            DMA((1,)), DMA((1,)),
        ],
        compiler_params=pltpu.CompilerParams(
            collective_id=0, has_side_effects=True, vmem_limit_bytes=63 * 2**20
        ),
    )(
        hidden_in,
        attn_gain.reshape(-1, 128),
        mlp_gain.reshape(-1, 128),
        lengths,
        w_query,
        w_key.T,
        w_value.T,
        w_out,
        w_gate.T,
        w_up.T,
        w_down,
        key_cache.reshape(4, slots, HD),
        value_cache.reshape(4, slots, HD),
    )


def solution(mesh):
    return jax.shard_map(
        on_device,
        mesh=mesh,
        in_specs=(
            P("hidden", "width"),
            P("width"),
            P("width"),
            P("width", "hidden"),
            P("width", "hidden"),
            P("width", "hidden"),
            P("hidden", "width"),
            P("width", "hidden"),
            P("width", "hidden"),
            P("hidden", "width"),
            P(("width", "hidden"), None, None, None),
            P(("width", "hidden"), None, None, None),
            P(("width", "hidden")),
        ),
        out_specs=P("hidden", "width"),
        check_vma=False,
    )
```

time: 171 us -> 160 us (0.936)
  Pallas kernels: 165 us -> 157 us
    pallas_call x1, Pallas kernels: 165 us -> 157 us  [on_device(): pl.pallas_call(layer_kernel, out_shape=jax.ShapeDtypeStruct(hidden_in.sha...]
where the time goes in v4:
time: 160 us; the launch traced here: 159 us
  Pallas kernels  157 us (98%)
    pallas_call x1, Pallas kernels, on_device(): pl.pallas_call(layer_kernel, out_shape=jax.ShapeDtypeStruct(hidden_in.sha...  157 us

profile of v4, /device:TPU:0, one launch (start us, length us, event | category | flops | bytes accessed | tf_op | source)
XLA Modules:
  0.0 158.6 jit_solution(9113233708183808341)
XLA Ops:
  0.0 157.0 %shard_map.127 = bf16[16,4096]{1,0:T(8,128)(2,1)} custom-call(bf16[16,4096]{1,0:T(8,128)(2,1)} %hidden_ref.1, bf16[32,128]{1,0:T(8,128)(2,1)} %bitcast.14, bf16[32,128]{1,0:T(8,128)(2,1)} %bitcast.15, s32[4]{0:T(128)} %lengths.1, bf16[4096,256]{1,0:T(8,128)(2,1)} %wq_hbm.1, bf16[16,4096]{1,0:T(8,128)(2,1)} %bitcast.12, bf16[16,4096]{1,0:T(8,128)(2,1)} %bitcast.13, ...), custom_call_target="tpu_custom_call" | custom-call | tf_op jit(solution)/shard_map/pallas_call | solution.py:769
  157.0 1.6 copy.15

commit v5 on v4

--- a/solution.py
+++ b/solution.py
@@ -50,7 +50,8 @@
 
 def enter(at):
     barrier = pltpu.get_barrier_semaphore()
-    peers = [at.core_peer, at.y_peer, at.far_peer] + [at.along(i) for i in range(1, 32)]
+    peers = [at.core_peer, at.y_peer, at.partner]
+    peers += [at.neighbour(f, 0, places) for f in (0, 1) for places in (1, -1, 2)]
     for peer in peers:
         pl.semaphore_signal(barrier, inc=1, device_id=peer, device_id_type=MESH)
     pl.semaphore_wait(barrier, len(peers))
@@ -159,13 +160,13 @@
         for j in OFFS:
             self.wait(1, j, 0, j, 2, self.way(j))
 
-    def tasks(self, add, name):
-        add(f"{name}.start", self.start)
-        add(f"{name}.first", self.first)
-        add(f"{name}.second", self.second)
-        add(f"{name}.third", self.third)
+    def tasks(self, add):
+        add(self.start)
+        add(self.first)
+        add(self.second)
+        add(self.third)
         for j in (0, -self.s, self.s, 2):
-            add(f"{name}.relay{j}", functools.partial(self.relay, j))
+            add(functools.partial(self.relay, j))
 
 
 class Scatter:
@@ -221,17 +222,17 @@
             value = value + self.take(0, 0, d, sgn)
         return value
 
-    def tasks(self, add, name):
+    def tasks(self, add):
         order = (2, -self.s, self.s, 0)
         for j in order:
-            add(f"{name}.far{j}", functools.partial(self.far, j), 0.06)
+            add(functools.partial(self.far, j), 0.06)
         for j in order:
-            add(f"{name}.back{j}", functools.partial(self.back, j), 0.06)
+            add(functools.partial(self.back, j), 0.06)
         for j in order:
-            add(f"{name}.on{j}", functools.partial(self.on, j), 0.08)
-        add(f"{name}.line_far", self.line_far, 0.1)
-        add(f"{name}.line_back", self.line_back, 0.1)
-        add(f"{name}.line_on", self.line_on, 0.1)
+            add(functools.partial(self.on, j), 0.08)
+        add(self.line_far, 0.1)
+        add(self.line_back, 0.1)
+        add(self.line_on, 0.1)
 
 
 def dot_nn(a, b):
@@ -365,10 +366,10 @@
     pairs = ((gss, grs), (ssem, rsem), (yss, yrs), (wss, wrs), (ass, ars), (bss, brs))
     glink, link, ylink, wlink, alink, blink = (Link(a, b, at.partner) for a, b in pairs)
     c_, yl = at.core, at.yl
-    tasks = {}
-
-    def add(name, body, cost=0.0):
-        tasks[name] = (body, cost)
+    tasks = []
+
+    def add(body, cost=0.0):
+        tasks.append((body, cost))
 
     def here(c):
         return (at.yh, c)
@@ -382,7 +383,7 @@
             wgu[k, pl.ds(units, 64), :] = jnp.zeros((64, width), BF16)
         wd[pl.ds(units, 64), :] = jnp.zeros((64, width), BF16)
 
-    add("zeros", fresh_zeros, 0.6)
+    add(fresh_zeros, 0.6)
 
     def swap_hidden():
         mine = hid.at[at.yh]
@@ -392,23 +393,22 @@
         theirs = hid.at[1 - at.yh]
         ylink.wait(8, theirs, at.partner)
 
-    add("zh_send", swap_hidden)
-    add("zh_wait", hidden_there)
-
-    def add_loaded(name, which):
+    add(swap_hidden)
+    add(hidden_there)
+
+    def add_loaded(which):
         def body():
             for load in which:
                 load.wait()
 
-        add(name, body)
-
-    add_loaded("load_qkv", loads[:3])
-    add_loaded("load_cache", loads[3:5])
-    add_loaded("load_out", loads[5:6])
-    add_loaded("load_mlp", loads[6:])
+        add(body)
+
+    add_loaded(loads[:3])
+    add_loaded(loads[3:5])
+    add_loaded(loads[5:6])
+    add_loaded(loads[6:])
 
     def add_gather(turn, c):
-        name = f"g{turn}{c}"
         halves = [Gather(at, glink, g, c, f) for f in (0, 1)]
 
         def slot(f):
@@ -424,18 +424,18 @@
             fill_own(g, at.block(c, 0, 0, 0), res[c].astype(F32), gain1[...].astype(F32), f)
 
         if turn == 0:
-            add(f"{name}.own", lambda: only(here(c), own_rows))
+            add(lambda: only(here(c), own_rows))
         else:
             for f in (0, 1):
-                add(f"{name}.{f}.own", functools.partial(new_rows, f), 0.2)
+                add(functools.partial(new_rows, f), 0.2)
         for f in (0, 1):
             def arrive(f=f):
                 theirs = g.at[at.partner[1], :, halves[f].cols]
                 only(there(c), lambda: ylink.wait(slot(f), theirs, at.partner))
 
             if turn == 0:
-                add(f"{name}.{f}.arrive", arrive)
-            halves[f].tasks(add, f"{name}.{f}")
+                add(arrive)
+            halves[f].tasks(add)
 
         def finish():
             for f in (0, 1):
@@ -443,15 +443,14 @@
             only(here(c), lambda: ylink.finish([slot(0), slot(1)], c))
 
         for f in (0, 1):
-            add(f"{name}.{f}.end", halves[f].end)
+            add(halves[f].end)
         if turn == 0:
-            add(f"{name}.finish", finish)
+            add(finish)
 
     def add_scatter(turn, c):
-        name = f"s{turn}{c}"
         for f in (0, 1):
             one = Scatter(at, link, acc, sbuf, rbuf, c, f)
-            one.tasks(add, f"{name}.{f}")
+            one.tasks(add)
             slot = 4 + c * 2 + f if turn == 0 else 9 + f
             buf = c * 2 + f if turn == 0 else 4 + f
             cols = pl.ds(f * half, half)
@@ -482,10 +481,10 @@
                 else:
                     only(here(c), body)
 
-            add(f"{name}.{f}.total", total, 0.15)
-            add(f"{name}.{f}.last", last, 0.1)
+            add(total, 0.15)
+            add(last, 0.1)
             if turn == 0:
-                add(f"{name}.{f}.finish", functools.partial(link.finish, slots_of(c, f)))
+                add(functools.partial(link.finish, slots_of(c, f)))
 
     def add_attention(c):
         active, passive = (at.yl, c), (at.yl, 1 - c)
@@ -582,15 +581,15 @@
                 acc[pl.ds(c * 16, 16), :, cols] = dot_nn(rows, wo[:, cols]).reshape(16, 16, 1024)
 
         for f in (0, 1):
-            add(f"a{c}.project{f}", functools.partial(project, f), 0.1 * f)
-        add(f"a{c}.over", over_y, 0.25)
-        add(f"a{c}.sum", lambda: only(active, sum_up), 1.0)
-        add(f"a{c}.attend", lambda: only(active, attention), 1.2)
-        add(f"a{c}.hand", lambda: only(active, hand_out), 0.3)
-        add(f"a{c}.take", take_in)
-        add(f"a{c}.other", take_other)
+            add(functools.partial(project, f), 0.1 * f)
+        add(over_y, 0.25)
+        add(lambda: only(active, sum_up), 1.0)
+        add(lambda: only(active, attention), 1.2)
+        add(lambda: only(active, hand_out), 0.3)
+        add(take_in)
+        add(take_other)
         for f in (0, 1):
-            add(f"a{c}.out{f}", functools.partial(out_product, f))
+            add(functools.partial(out_product, f))
 
     def add_mlp(c):
         cuts = ((0, 256), (256, 256), (512, 384))
@@ -659,13 +658,13 @@
         for i in (2, 0, 1):
             for k in (0, 1):
                 for f in (0, 1):
-                    add(f"m{c}.gu{k}{i}{f}", functools.partial(gate_up, k, i, f), 0.03 + 0.06 * f)
-                add(f"m{c}.y{k}{i}", functools.partial(over_y, k, i), 0.07)
-            add(f"m{c}.act{i}", functools.partial(activate, i), 0.2)
-            add(f"m{c}.pass{i}", functools.partial(pass_on, i))
-        add(f"m{c}.complete", complete)
+                    add(functools.partial(gate_up, k, i, f), 0.03 + 0.06 * f)
+                add(functools.partial(over_y, k, i), 0.07)
+            add(functools.partial(activate, i), 0.2)
+            add(functools.partial(pass_on, i))
+        add(complete)
         for i in range(4):
-            add(f"m{c}.down{i}", functools.partial(down, i))
+            add(functools.partial(down, i))
 
     for c in (0, 1):
         add_gather(0, c)
@@ -675,9 +674,8 @@
         add_mlp(c)
         add_scatter(1, c)
 
-    for name in order_of(tasks):
-        enter_task(name, tasks[name][1])
-        tasks[name][0]()
+    for place in ORDER:
+        tasks[place][0]()
     for each in (glink, link, ylink, wlink):
         each.finish()
     for c in (0, 1):
@@ -685,61 +683,22 @@
         only((at.yl, c), lambda c=c: wlink.finish(None, c))
 
 
-def enter_task(name, cost):
-    pass
-
-
 ORDER = [
-    "load_qkv", "g01.own", "load_cache", "g00.own", "g00.0.arrive", "g00.0.start", "g00.1.arrive",
-    "g00.1.start", "g01.0.arrive", "g01.0.start", "g00.0.first", "g00.1.second", "g00.0.second",
-    "g00.1.first", "g00.0.third", "g00.0.relay0", "g00.0.relay-1", "g00.1.third", "g01.1.arrive",
-    "g01.1.start", "g00.1.relay-1", "g00.0.relay1", "g00.1.relay0", "g00.0.relay2", "g00.1.relay1",
-    "g01.0.third", "g00.1.relay2", "zeros", "g01.1.relay0", "g01.1.first", "load_mlp", "g01.0.second",
-    "g01.1.second", "g01.0.first", "g00.0.end", "a0.project0", "g00.1.end", "a0.project1", "g01.1.third",
-    "a0.over", "g01.0.relay0", "g01.0.relay2", "zh_send", "g01.0.relay-1", "g01.1.relay1", "g01.0.relay1",
-    "load_out", "g01.1.relay-1", "g01.1.relay2", "a0.sum", "g00.finish", "g01.0.end", "a1.project0",
-    "g01.1.end", "a1.project1", "a1.over", "a0.attend", "a1.sum", "a0.hand", "a1.attend", "a0.take",
-    "a0.other", "a0.out0", "s00.0.far2", "a0.out1", "s00.1.far0", "s00.1.far2", "s00.0.far1", "s00.0.back-1",
-    "g01.finish", "s00.1.back0", "s00.0.far-1", "s00.1.far1", "s00.0.far0", "a1.hand", "s00.1.far-1",
-    "s00.0.back1", "s00.1.back2", "s00.0.on2", "s00.1.on0", "s00.1.on2", "s00.0.back2", "s00.1.back1",
-    "s00.0.on1", "s00.1.on1", "s00.0.on-1", "s00.1.back-1", "s00.0.back0", "s00.0.on0", "s00.1.on-1",
-    "a1.take", "a1.other", "a1.out0", "s01.0.far1", "a1.out1", "s00.0.line_far", "s01.1.far2", "s01.0.far2",
-    "s01.0.far-1", "s00.0.line_on", "s00.1.line_far", "s01.1.far-1", "s00.1.line_back", "s00.0.line_back",
-    "s00.1.line_on", "s01.1.far1", "s01.1.far0", "s01.1.back2", "s01.0.back0", "s01.0.far0", "s01.1.back-1",
-    "s01.1.on2", "s01.0.on2", "s01.0.back1", "s01.0.back2", "s01.0.on1", "s00.0.total", "s01.0.on-1",
-    "s01.1.on1", "s01.1.back0", "s01.1.on-1", "s00.1.total", "s01.1.back1", "s01.0.back-1", "s01.0.on0",
-    "s01.1.on0", "s01.0.line_far", "s01.1.line_far", "zh_wait", "s01.0.line_back", "s01.1.line_back",
-    "s01.0.line_on", "s01.1.line_on", "s00.0.last", "g10.0.own", "g10.0.start", "s00.1.last", "g10.1.own",
-    "g10.1.start", "s01.0.total", "g10.0.second", "g10.0.first", "s01.1.total", "g10.1.first", "g10.0.third",
-    "g10.1.second", "g10.0.relay0", "g10.1.third", "g10.0.relay-1", "s01.0.last", "g11.0.own", "g11.0.start",
-    "g10.0.relay1", "s01.1.last", "g10.1.relay0", "g11.1.own", "g10.1.relay1", "g10.0.relay2", "g11.1.start",
-    "g10.1.relay-1", "g10.1.relay2", "g11.0.second", "g10.0.end", "g11.0.third", "g11.1.relay0",
-    "g11.0.first", "m0.gu120", "m0.gu000", "g11.1.first", "g11.1.second", "m0.gu020", "s00.1.finish",
-    "m0.gu100", "g10.1.end", "m0.gu121", "g11.1.third", "s00.0.finish", "m0.gu021", "g11.0.relay-1",
-    "g11.0.relay0", "m0.y12", "m0.gu101", "m0.gu001", "g11.0.relay2", "m0.y02", "g11.0.relay1", "m0.gu110",
-    "m0.gu010", "m0.gu011", "s01.0.finish", "m0.y10", "m0.gu111", "g11.1.relay1", "m0.y00", "m0.y01",
-    "g11.1.relay-1", "m0.y11", "g11.1.relay2", "m0.act2", "g11.0.end", "m1.gu110", "m1.gu010", "m1.gu000",
-    "m1.gu020", "m0.act0", "m1.gu120", "m0.act1", "g11.1.end", "m1.gu111", "m1.gu021", "m1.gu121", "m1.y11",
-    "m1.gu011", "m1.y02", "m1.gu001", "m0.pass1", "m0.pass2", "m0.pass0", "s01.1.finish", "m1.y12",
-    "m1.gu100", "m1.gu101", "m1.y01", "m1.y00", "m0.complete", "m0.down1", "m1.y10", "m0.down0", "s10.0.far1",
-    "s10.0.far0", "m0.down2", "m0.down3", "s10.1.far2", "m1.act2", "s10.0.far-1", "s10.1.far0", "s10.0.far2",
-    "s10.1.far-1", "m1.act1", "s10.1.far1", "s10.0.back2", "s10.0.back-1", "s10.0.back1", "m1.act0",
-    "s10.1.back-1", "s10.1.back1", "s10.1.back2", "s10.0.on1", "s10.1.back0", "m1.pass1", "s10.0.on-1",
-    "s10.1.on2", "s10.0.back0", "m1.pass0", "m1.pass2", "s10.1.on0", "s10.0.on0", "s10.1.on1", "s10.0.on2",
-    "s10.1.on-1", "m1.complete", "m1.down0", "m1.down1", "s11.0.far2", "s11.0.far1", "m1.down3", "m1.down2",
-    "s11.1.far2", "s11.1.far-1", "s11.0.far-1", "s11.0.back2", "s11.0.back0", "s11.1.far0", "s11.0.far0",
-    "s10.1.line_far", "s11.1.back2", "s11.1.far1", "s11.1.back-1", "s10.1.line_on", "s10.1.line_back",
-    "s11.0.back-1", "s11.0.back1", "s11.0.on1", "s10.0.line_on", "s11.0.on2", "s11.1.on2", "s11.1.on-1",
-    "s11.1.on1", "s11.1.back1", "s10.0.line_far", "s10.0.line_back", "s11.1.on0", "s11.1.back0", "s11.0.on0",
-    "s11.0.on-1", "s11.1.line_far", "s11.0.line_far", "s10.1.total", "s11.1.line_on", "s11.1.line_back",
-    "s11.0.line_on", "s11.0.line_back", "s10.0.total", "s11.1.total", "s11.0.total", "s10.1.last",
-    "s11.1.last", "s10.0.last", "s11.0.last",
+    7, 158, 8, 9, 17, 18, 159, 160, 1, 10, 11, 6, 19, 12, 20, 21, 168, 13, 14, 169, 15, 23, 5, 24, 0, 16, 22,
+    3, 162, 25, 161, 171, 163, 173, 170, 164, 26, 29, 27, 30, 172, 175, 31, 165, 166, 4, 167, 174, 176, 32,
+    177, 180, 178, 181, 182, 33, 183, 28, 34, 184, 35, 36, 37, 41, 38, 57, 60, 40, 58, 61, 179, 39, 42, 46,
+    59, 63, 45, 43, 62, 185, 49, 65, 47, 44, 64, 67, 66, 48, 68, 50, 53, 186, 187, 69, 188, 189, 192, 208,
+    190, 51, 52, 71, 209, 210, 193, 213, 191, 211, 70, 216, 2, 212, 200, 196, 198, 54, 215, 72, 194, 195, 217,
+    197, 218, 214, 219, 199, 201, 204, 220, 202, 221, 203, 222, 55, 75, 77, 73, 76, 85, 205, 223, 79, 78, 86,
+    87, 81, 80, 89, 88, 83, 82, 206, 226, 228, 224, 227, 90, 84, 91, 236, 230, 92, 93, 237, 95, 111, 231, 106,
+    98, 238, 229, 94, 96, 103, 99, 239, 97, 234, 232, 74, 225, 112, 104, 100, 235, 114, 233, 107, 105, 241,
+    242, 115, 113, 240, 108, 243, 116, 101, 244, 246, 249, 254, 109, 117, 245, 250, 262, 247, 265, 251, 255,
+    102, 263, 110, 248, 257, 118, 258, 256, 207, 266, 264, 119, 122, 259, 123, 267, 143, 147, 56, 121, 120,
+    126, 252, 124, 141, 144, 127, 260, 125, 148, 142, 268, 129, 146, 151, 145, 128, 131, 253, 261, 135, 152,
+    149, 269, 134, 132, 130, 150, 133, 270, 274, 273, 294, 298, 271, 272, 275, 276, 296, 292, 293, 277, 297,
+    282, 295, 278, 138, 279, 155, 302, 281, 137, 283, 136, 284, 153, 300, 285, 301, 280, 154, 286, 299, 303,
+    287, 306, 304, 289, 288, 139, 305, 156, 290, 291, 307, 140, 157, 308,
 ]
-
-
-def order_of(tasks):
-    assert sorted(ORDER) == sorted(tasks)
-    return ORDER
 
 
 VM = pl.BlockSpec(memory_space=pltpu.VMEM)

time: 160 us -> 156 us (0.975)
  Pallas kernels: 157 us -> 154 us
    pallas_call x1, Pallas kernels: 157 us -> 154 us  [on_device(): pl.pallas_call(layer_kernel, out_shape=jax.ShapeDtypeStruct(hidden_in.sha...]
where the time goes in v5:
time: 156 us; the launch traced here: 155 us
  Pallas kernels  154 us (99%)
  local copies, waits for them, and re-layouts  1.57 us (1%)
    pallas_call x1, Pallas kernels, on_device(): pl.pallas_call(layer_kernel, out_shape=jax.ShapeDtypeStruct(hidden_in.sha...  154 us

profile of v5, /device:TPU:0, one launch (start us, length us, event | category | flops | bytes accessed | tf_op | source)
XLA Modules:
  0.0 155.4 jit_solution(9863306880895729609)
XLA Ops:
  0.0 153.8 %shard_map.127 = bf16[16,4096]{1,0:T(8,128)(2,1)} custom-call(bf16[16,4096]{1,0:T(8,128)(2,1)} %hidden_ref.1, bf16[32,128]{1,0:T(8,128)(2,1)} %bitcast.14, bf16[32,128]{1,0:T(8,128)(2,1)} %bitcast.15, s32[4]{0:T(128)} %lengths.1, bf16[4096,256]{1,0:T(8,128)(2,1)} %wq_hbm.1, bf16[16,4096]{1,0:T(8,128)(2,1)} %bitcast.12, bf16[16,4096]{1,0:T(8,128)(2,1)} %bitcast.13, ...), custom_call_target="tpu_custom_call" | custom-call | tf_op jit(solution)/shard_map/pallas_call | solution.py:728
  153.8 1.6 %copy.15 = bf16[16,4096]{1,0:T(8,128)(2,1)} copy(bf16[16,4096]{1,0:T(8,128)(2,1)} %shard_map.127) | data formatting | bytes 262144

commit v6 on v5

--- a/solution.py
+++ b/solution.py
@@ -48,13 +48,13 @@
         return (self.w, lax.rem(self.h + i, 32))
 
 
-def enter(at):
+def greet(at):
     barrier = pltpu.get_barrier_semaphore()
     peers = [at.core_peer, at.y_peer, at.partner]
     peers += [at.neighbour(f, 0, places) for f in (0, 1) for places in (1, -1, 2)]
     for peer in peers:
         pl.semaphore_signal(barrier, inc=1, device_id=peer, device_id_type=MESH)
-    pl.semaphore_wait(barrier, len(peers))
+    return lambda: pl.semaphore_wait(barrier, len(peers))
 
 
 class Link:
@@ -338,6 +338,7 @@
     lsem, gss, grs, ssem, rsem, yss, yrs, wss, wrs, ass, ars, bss, brs,
 ):
     at = Place()
+    enter = greet(at)
     width = hidden_ref.shape[1]
     units = wd_hbm.shape[0]
     half = width // 2
@@ -362,7 +363,7 @@
     hid[at.yh] = hidden_ref[...]
     for f in (0, 1):
         fill_own(g, at.h, hidden_ref[...].astype(F32), gain0[...].astype(F32), f)
-    enter(at)
+    enter()
     pairs = ((gss, grs), (ssem, rsem), (yss, yrs), (wss, wrs), (ass, ars), (bss, brs))
     glink, link, ylink, wlink, alink, blink = (Link(a, b, at.partner) for a, b in pairs)
     c_, yl = at.core, at.yl

time: 156 us -> 156 us (level)
  no operation moved by 1% of the time
where the time goes in v6:
time: 156 us; the launch traced here: 155 us
  Pallas kernels  154 us (99%)
  local copies, waits for them, and re-layouts  1.57 us (1%)
    pallas_call x1, Pallas kernels, on_device(): pl.pallas_call(layer_kernel, out_shape=jax.ShapeDtypeStruct(hidden_in.sha...  154 us

profile of v6, /device:TPU:0, one launch (start us, length us, event | category | flops | bytes accessed | tf_op | source)
XLA Modules:
  0.0 155.3 jit_solution(5444674003753861972)
XLA Ops:
  0.0 153.7 %shard_map.127 = bf16[16,4096]{1,0:T(8,128)(2,1)} custom-call(bf16[16,4096]{1,0:T(8,128)(2,1)} %hidden_ref.1, bf16[32,128]{1,0:T(8,128)(2,1)} %bitcast.14, bf16[32,128]{1,0:T(8,128)(2,1)} %bitcast.15, s32[4]{0:T(128)} %lengths.1, bf16[4096,256]{1,0:T(8,128)(2,1)} %wq_hbm.1, bf16[16,4096]{1,0:T(8,128)(2,1)} %bitcast.12, bf16[16,4096]{1,0:T(8,128)(2,1)} %bitcast.13, ...), custom_call_target="tpu_custom_call" | custom-call | tf_op jit(solution)/shard_map/pallas_call | solution.py:729
  153.7 1.6 %copy.15 = bf16[16,4096]{1,0:T(8,128)(2,1)} copy(bf16[16,4096]{1,0:T(8,128)(2,1)} %shard_map.127) | data formatting | bytes 262144
